TPU v7x, 512 devices: a whole 4x8x8 slice. The times are simulated.
512 devices in a mesh: dom: 128 (over z_hi, x, y), edge: 4 (over z_lo, core).
Axes of the slice: x: 4, y: 8, z: 8 (z_hi: 4, z_lo: 2; z = z_hi * 2 + z_lo), core: 2. Of those that a mesh axis runs over, the one named last changes fastest.
Arguments:
- embeddings: float32 [400, 65536], P(None, 'dom'), may hold values from -1.2 to 1.2
- accum: float32 [65536], P('dom'), may hold values from 0.01 to 1
- relations: float32 [400, 1024], replicated, may hold values from -6 to 6
- rel_accum: float32 [1024], replicated, may hold values from 0.01 to 1
- src_ids: int32 [128, 4096], P('dom', 'edge'), may hold values from 0 to 511
- rel_ids: int32 [128, 4096], P('dom', 'edge'), may hold values from 0 to 1023
- dst_ids: int32 [128, 4096], P('dom', 'edge'), may hold values from 0 to 511
- neg_ids: int32 [128, 8, 1024], P('dom', 'edge'), may hold values from 0 to 511
- bucket_len: int32 [128], P('dom'), may hold values from 512 to 4096, as said below
- partner: int32 [128], replicated, may hold values from 0 to 127, as said below
Outputs:
- new_embeddings: float32 [400, 65536], P(None, 'dom')
- new_accum: float32 [65536], P('dom')
- new_relations: float32 [400, 1024], replicated
- new_rel_accum: float32 [1024], replicated
Inputs may be any that keep to these rules, and one draw needn't show every extreme that they name: The live slots of bucket d are its first bucket_len[d] slots; some bucket is full in every draw. partner[partner[d]] == d and partner[d] != d for every d.
All inputs are finite; a program needn't handle non-finite values.
Results may differ from a plain program's by a relative error of at most 0.0003.
The roundings to bfloat16 on the way count: a program that leaves them out, or rounds other values in their place, can miss the bound.
Values may be sent and summed in bfloat16 or wider, within the bound.
A program may use at most 64 MiB of HBM per device.

v0:
```python
import jax
import jax.numpy as jnp
from jax import lax
from jax.sharding import PartitionSpec as P

learn_rate = 0.1


def relay(block, partner, first_leg, second_leg):
    count = partner.shape[0]
    flat = block.reshape(count, -1)
    spread = first_leg(flat)
    routed = jnp.take(spread, partner, axis=0)
    return second_leg(routed).reshape(block.shape)


def spread_columns(values, indices, total):
    onehot = (indices[:, None] == jnp.arange(total, dtype=jnp.int32)[None, :]).astype(jnp.float32)
    return jnp.dot(
        values, onehot, precision=lax.Precision.HIGHEST, preferred_element_type=jnp.float32
    )


def bucket_terms(own_b, other_b, relations, src, rel, dst, neg, live):
    dim = own_b.shape[0]
    half = dim // 2
    edges = src.shape[0]
    blocks, negcount = neg.shape
    width = edges // blocks
    h = jnp.take(own_b, src, axis=1).astype(jnp.float32)
    t = jnp.take(other_b, dst, axis=1).astype(jnp.float32)
    r = jnp.take(relations, rel, axis=1)
    h_re, h_im = (h[:half], h[half:])
    r_re, r_im = (r[:half], r[half:])
    q = jnp.concatenate([h_re * r_re - h_im * r_im, h_re * r_im + h_im * r_re], axis=0)
    pos = jnp.sum(q * t, axis=0)
    q_b = q.astype(jnp.bfloat16)
    neg_flat = neg.reshape(-1)
    neg_cols = jnp.take(other_b, neg_flat, axis=1).reshape(dim, blocks, negcount)
    q_blocks = q_b.reshape(dim, blocks, width)
    negs = jnp.einsum("dkb,dkn->kbn", q_blocks, neg_cols, preferred_element_type=jnp.float32)
    live_blocks = live.reshape(blocks, width)
    g_pos = -live * jax.nn.sigmoid(-pos)
    g_neg = (live_blocks[:, :, None] * jax.nn.sigmoid(negs) / negcount**0.5).astype(jnp.bfloat16)
    back = jnp.einsum("dkn,kbn->dkb", neg_cols, g_neg, preferred_element_type=jnp.float32).reshape(
        dim, edges
    )
    dq = t * g_pos + back
    dt = q * g_pos
    dn = jnp.einsum("dkb,kbn->dkn", q_blocks, g_neg, preferred_element_type=jnp.float32).reshape(
        dim, blocks * negcount
    )
    dq_re, dq_im = (dq[:half], dq[half:])
    dh = jnp.concatenate([dq_re * r_re + dq_im * r_im, dq_im * r_re - dq_re * r_im], axis=0)
    dr = jnp.concatenate([dq_re * h_re + dq_im * h_im, dq_im * h_re - dq_re * h_im], axis=0)
    ent = own_b.shape[1]
    g_own = spread_columns(dh, src, ent)
    g_other = spread_columns(
        jnp.concatenate([dt, dn], axis=1), jnp.concatenate([dst, neg_flat], axis=0), ent
    )
    g_rel = spread_columns(dr, rel, relations.shape[1])
    return (g_own, g_other, g_rel)


def shards(
    embeddings, accum, relations, rel_accum, src_ids, rel_ids, dst_ids, neg_ids, bucket_len, partner
):
    member = lax.axis_index("edge")
    edges = src_ids.shape[1]
    position = member * edges + jnp.arange(edges, dtype=jnp.int32)
    live = (position < bucket_len[0]).astype(jnp.float32)
    own_b = embeddings.astype(jnp.bfloat16)
    other_b = relay(
        own_b,
        partner,
        lambda value: lax.all_to_all(value, "dom", split_axis=0, concat_axis=0, tiled=True),
        lambda value: lax.all_to_all(value, "dom", split_axis=0, concat_axis=0, tiled=True),
    )
    g_own, g_other, g_rel = bucket_terms(
        own_b, other_b, relations, src_ids[0], rel_ids[0], dst_ids[0], neg_ids[0], live
    )
    rel_total = lax.psum(g_rel, ("dom", "edge"))
    new_rel_accum = rel_accum + jnp.mean(rel_total * rel_total, axis=0)
    new_relations = relations - learn_rate * rel_total / jnp.sqrt(new_rel_accum)
    returned = relay(
        g_other,
        partner,
        lambda value: lax.all_to_all(value, "dom", split_axis=0, concat_axis=0, tiled=True),
        lambda value: lax.all_to_all(value, "dom", split_axis=0, concat_axis=0, tiled=True),
    )
    total = lax.psum(g_own + returned, "edge")
    new_accum = accum + jnp.mean(total * total, axis=0)
    new_embeddings = embeddings - learn_rate * total / jnp.sqrt(new_accum)
    return (new_embeddings, new_accum, new_relations, new_rel_accum)


def solution(mesh):
    return jax.shard_map(
        shards,
        mesh=mesh,
        in_specs=(
            P(None, "dom"),
            P("dom"),
            P(),
            P(),
            P("dom", "edge"),
            P("dom", "edge"),
            P("dom", "edge"),
            P("dom", "edge", None),
            P("dom"),
            P(),
        ),
        out_specs=(P(None, "dom"), P("dom"), P(), P()),
        check_vma=False,
    )
```

profile of v0, /device:TPU:1, one launch (start us, length us, event | category | flops | bytes accessed | tf_op | source)
XLA Modules:
  0.0 541.6 jit_solution(2183450644291612493)
XLA Ops:
  7.2 1.2 convert_element_type.30
  8.4 0.7 all_to_all.32
  9.0 0.5 broadcast.197
  9.6 3.3 reduce.2
  12.9 1.2 reshape.261
  14.1 21.3 %all-to-all-start = ((bf16[128,2,800]{2,1,0:T(2,128)(2,1)}), bf16[128,2,800]{2,1,0:T(2,128)(2,1)}, u32[]{:S(2)}, u32[]{:S(2)}) async-start(bf16[128,2,800]{2,1,0:T(2,128)(2,1)} %reshape.261), calls=%async_computation | async-start | bytes 917504 | tf_op jit(solution)/shard_map/all_to_all | solution.py:76
  35.4 0.2 copy.81
  35.7 4.0 gather_fusion.5
  39.7 1.2 copy.82
  40.9 1.8 copy.83
  42.8 4.9 gather_fusion.1
  47.7 1.9 copy.84
  50.4 1.3 bitcast_convert_fusion
  51.7 1.3 select_bitcast_fusion
  52.9 0.9 all-to-all-done
  53.9 3.1 reshape.262
  57.0 0.1 copy.109
  57.0 1.7 gather_fusion
  58.7 2.0 bitcast_select_fusion.1
  60.7 2.6 reduce.3
  63.3 2.2 reshape.263
  65.5 15.3 %all-to-all-start.1 = ((bf16[128,2,800]{2,1,0:T(2,128)(2,1)}), bf16[128,2,800]{2,1,0:T(2,128)(2,1)}, u32[]{:S(2)}, u32[]{:S(2)}) async-start(bf16[128,2,800]{2,1,0:T(2,128)(2,1)} %reshape.263), calls=%async_computation.1 | async-start | bytes 917504 | tf_op jit(solution)/shard_map/all_to_all | solution.py:77
  80.9 1.6 fusion.32
  82.5 16.1 %all-to-all-done.1 = bf16[128,2,800]{2,1,0:T(2,128)(2,1)} async-done(((bf16[128,2,800]{2,1,0:T(2,128)(2,1)}), bf16[128,2,800]{2,1,0:T(2,128)(2,1)}, u32[]{:S(2)}, u32[]{:S(2)}) %all-to-all-start.1) | async-done | bytes 409632 | tf_op jit(solution)/shard_map/all_to_all | solution.py:77
  98.6 3.1 reshape.264
  101.7 3.4 reduce
  105.1 2.4 reshape.199
  107.5 1.2 copy.79
  108.7 9.2 %gather_fusion.2 = bf16[2048,400]{1,0:T(8,128)(2,1)} fusion(bf16[400,512]{0,1:T(8,128)(2,1)S(1)} %copy.79, s32[2048]{0:T(1024)S(1)} %broadcast_clamp_fusion), kind=kCustom, calls=%fused_computation.4 | custom fusion | bytes 3284992 | tf_op jit(solution)/shard_map/jit(_take)/gather | solution.py:39
  118.0 3.9 copy.88
  121.9 3.5 multiply_convert_fusion
  125.3 1.0 convolution_bitcast_fusion.1
  126.4 2.7 convolution_bitcast_fusion
  129.1 1.3 copy.99
  130.5 4.0 gather_fusion.4
  134.4 0.7 copy.80
  135.2 2.3 copy.100
  137.5 0.1 copy-done.3
  137.5 0.3 fusion.8
  137.8 1.1 copy-done.4
  138.9 1.8 fusion.9
  140.7 4.7 fusion
  145.4 1.2 all_to_all.33
  146.6 34.3 %all_to_all.38 = f32[128,1,1600]{2,1,0:T(1,128)S(1)} all-to-all(f32[128,1,1600]{2,1,0:T(1,128)S(1)} %all_to_all.33), channel_id=1, replica_groups=mesh['dom'=128,'edge'=4] {'dom'}, dimensions={0} | all-to-all | bytes 1638400 | tf_op jit(solution)/shard_map/all_to_all | solution.py:88
  180.9 0.1 copy.108
  181.0 1.0 gather_fusion.3
  181.9 0.1 bitcast_select_fusion
  182.1 1.8 copy.94
  183.9 8.0 %all-to-all-start.3 = ((f32[128,1,1600]{2,1,0:T(1,128)}), f32[128,1,1600]{2,1,0:T(1,128)}, u32[]{:S(2)}, u32[]{:S(2)}) async-start(f32[128,1,1600]{2,1,0:T(1,128)} %copy.94), calls=%async_computation.3 | async-start | bytes 1703936 | tf_op jit(solution)/shard_map/all_to_all | solution.py:89
  191.9 0.3 all-reduce.5.cloned.1.call-start
  192.2 3.2 multiply_add_fusion
  195.4 4.3 fusion.4
  199.8 17.3 %all-to-all-done.3 = f32[128,1,1600]{2,1,0:T(1,128)} async-done(((f32[128,1,1600]{2,1,0:T(1,128)}), f32[128,1,1600]{2,1,0:T(1,128)}, u32[]{:S(2)}, u32[]{:S(2)}) %all-to-all-start.3) | async-done | bytes 819232 | tf_op jit(solution)/shard_map/all_to_all | solution.py:89
  217.1 3.2 reduce.1
  220.3 0.5 reshape.202
  220.8 2.6 fusion.17
  223.5 256.3 %all-reduce.5.cloned.1.call-done = f32[400,1024]{1,0:T(8,128)} async-done(((f32[400,1024]{1,0:T(8,128)}), f32[400,1024]{1,0:T(8,128)}) %all-reduce.5.cloned.1.call-update) | async-done | bytes 1638416 | tf_op jit(solution)/shard_map/psum | solution.py:82
  479.8 1.6 multiply_reduce_fusion
  481.3 0.6 fusion.30
  482.0 3.0 divide_subtract_fusion
  485.0 45.3 %all-reduce.3.cloned.1.call-done = f32[400,512]{1,0:T(8,128)} async-done(((f32[400,512]{1,0:T(8,128)}), f32[400,512]{1,0:T(8,128)}) %all-reduce.3.cloned.1.call-update) | async-done | bytes 819216 | tf_op jit(solution)/shard_map/psum | solution.py:91
  530.3 1.2 multiply_reduce_fusion.1
  531.6 0.6 fusion.31
  532.1 2.2 divide_subtract_fusion.1
  (54 shorter events, 0.3 us)
Async XLA Ops:
  12.9 22.8 %copy-start.11 = (s32[1,1024]{1,0:T(1,128)S(1)}, s32[1,1024]{1,0:T(1,128)}, u32[]{:S(2)}) copy-start(s32[1,1024]{1,0:T(1,128)} %param.16) | copy-start | bytes 12292
  12.9 22.8 %copy-start.12 = (s32[1,1024]{1,0:T(1,128)S(1)}, s32[1,1024]{1,0:T(1,128)}, u32[]{:S(2)}) copy-start(s32[1,1024]{1,0:T(1,128)} %param.18) | copy-start | bytes 12292
  14.1 39.7 %all-to-all-start = ((bf16[128,2,800]{2,1,0:T(2,128)(2,1)}), bf16[128,2,800]{2,1,0:T(2,128)(2,1)}, u32[]{:S(2)}, u32[]{:S(2)}) async-start(bf16[128,2,800]{2,1,0:T(2,128)(2,1)} %reshape.261), calls=%async_computation | async-start | bytes 917504 | tf_op jit(solution)/shard_map/all_to_all | solution.py:76
  39.7 1.2 copy-start.13
  47.7 1.9 copy-start.16
  47.7 1.9 copy-start.10
  58.7 22.2 %copy-start = (f32[400,1024]{1,0:T(8,128)S(1)}, f32[400,1024]{1,0:T(8,128)}, u32[]{:S(2)}) copy-start(f32[400,1024]{1,0:T(8,128)} %select_bitcast_fusion) | copy-start | bytes 4915204
  65.5 33.1 %all-to-all-start.1 = ((bf16[128,2,800]{2,1,0:T(2,128)(2,1)}), bf16[128,2,800]{2,1,0:T(2,128)(2,1)}, u32[]{:S(2)}, u32[]{:S(2)}) async-start(bf16[128,2,800]{2,1,0:T(2,128)(2,1)} %reshape.263), calls=%async_computation.1 | async-start | bytes 917504 | tf_op jit(solution)/shard_map/all_to_all | solution.py:77
  121.9 3.5 copy-start.9
  135.2 2.3 copy-start.2
  135.2 2.4 copy-start.3
  137.5 1.4 copy-start.4
  182.1 10.1 %copy-start.1 = (f32[400,1024]{1,0:T(8,128)S(1)}, f32[400,1024]{1,0:T(8,128)}, u32[]{:S(2)}) copy-start(f32[400,1024]{1,0:T(8,128)} %select_bitcast_fusion) | copy-start | bytes 4915204
  183.9 33.2 %all-to-all-start.3 = ((f32[128,1,1600]{2,1,0:T(1,128)}), f32[128,1,1600]{2,1,0:T(1,128)}, u32[]{:S(2)}, u32[]{:S(2)}) async-start(f32[128,1,1600]{2,1,0:T(1,128)} %copy.94), calls=%async_computation.3 | async-start | bytes 1703936 | tf_op jit(solution)/shard_map/all_to_all | solution.py:89
  191.9 287.9 %all-reduce.5.cloned.1.call-start = ((), (), s32[]{:S(2)}) async-start(), calls=%async_computation.5 | async-start | bytes 3276800 | tf_op jit(solution)/shard_map/psum | solution.py:82
  199.7 21.1 %copy-start.7 = (f32[200,1024]{1,0:T(8,128)S(1)}, f32[200,1024]{1,0:T(8,128)}, u32[]{:S(2)}) copy-start(f32[200,1024]{1,0:T(8,128)} %get-tuple-element.19) | copy-start | bytes 2457604
  199.7 21.1 %copy-start.8 = (f32[200,1024]{1,0:T(8,128)S(1)}, f32[200,1024]{1,0:T(8,128)}, u32[]{:S(2)}) copy-start(f32[200,1024]{1,0:T(8,128)} %get-tuple-element.20) | copy-start | bytes 2457604
  199.7 330.6 %all-reduce.3.cloned.1.call-start = ((), (), s32[]{:S(2)}) async-start(), calls=%async_computation.4 | async-start | bytes 1638400 | tf_op jit(solution)/shard_map/psum | solution.py:91
  223.5 257.9 %copy-start.14 = (f32[1024]{0:T(1024)S(1)}, f32[1024]{0:T(1024)}, u32[]{:S(2)}) copy-start(f32[1024]{0:T(1024)} %param.15) | copy-start | bytes 12292
  223.5 258.5 %copy-start.5 = (f32[400,1024]{1,0:T(8,128)S(1)}, f32[400,1024]{1,0:T(8,128)}, u32[]{:S(2)}) copy-start(f32[400,1024]{1,0:T(8,128)} %param.14) | copy-start | bytes 4915204
  481.9 49.6 %copy-start.15 = (f32[512]{0:T(512)S(1)}, f32[512]{0:T(512)}, u32[]{:S(2)}) copy-start(f32[512]{0:T(512)} %param.13) | copy-start | bytes 6148
  481.9 50.2 %copy-start.6 = (f32[400,512]{1,0:T(8,128)S(1)}, f32[400,512]{1,0:T(8,128)}, u32[]{:S(2)}) copy-start(f32[400,512]{1,0:T(8,128)} %param.12) | copy-start | bytes 2457604
Sparse Core Ops, SparseCore 0:
  199.8 279.8 all-reduce.4
  483.6 46.7 all-reduce.2
where the time goes:
time: 551 us; the launch traced here: 542 us
  waiting for transfers between devices  336 us (61%)
  local copies, waits for them, and re-layouts  57.4 us (10%)
  starting transfers between devices  44.9 us (8%)
  other arithmetic  34.7 us (6%)
  blocking collectives  34.3 us (6%)
  matrix products  18.8 us (3%)
  between operations  15.6 us (3%)
    psum x1, waiting for transfers between devices, shards(): rel_total = lax.psum(g_rel, ('dom', 'edge'))  256 us
    psum x1, waiting for transfers between devices, shards(): total = lax.psum(g_own + returned, 'edge')  45.3 us
    all_to_all x3, starting transfers between devices, shards(): lax.all_to_all(value, 'dom', split_axis=0, concat_axis=0, tiled=True)  44.6 us
    all_to_all x1, blocking collectives, shards(): lax.all_to_all(value, 'dom', split_axis=0, concat_axis=0, tiled=True)  34.3 us
    all_to_all x3, waiting for transfers between devices, shards(): lax.all_to_all(value, 'dom', split_axis=0, concat_axis=0, tiled=True)  34.3 us
    gather x2, local copies, waits for them, and re-layouts, bucket_terms(): jnp.take(other_b, neg_flat, axis=1).reshape(dim, blocks, negcount)  13.1 us
    unnamed x42, local copies, waits for them, and re-layouts  12.7 us
    dot_general x3, matrix products, spread_columns(): jnp.dot(values, onehot, precision=lax.Precision.HIGHEST, preferred_elemen...  11.6 us
  transfers between devices with their start and end apart: 5, of which 5 were waited for; matrix products, arithmetic and copies ran while one was open for 7% of the time, Pallas kernels for 0%

commit v1 on v0

v1 whole, which is shorter than its diff:
```python
import functools

import jax
import jax.numpy as jnp
from jax import lax
from jax.experimental import pallas as pl
from jax.experimental.pallas import tpu as pltpu
from jax.sharding import PartitionSpec as P

MESH = pl.DeviceIdType.MESH
VMEM = pl.BlockSpec(memory_space=pltpu.VMEM)
SMEM = pl.BlockSpec(memory_space=pltpu.SMEM)
f32, bf16, i32 = jnp.float32, jnp.bfloat16, jnp.int32
learn_rate = 0.1
DOM = 128
HUBS = 32
ID_TILES = 5


def remote(src, dst, send, recv, device):
    return pltpu.make_async_remote_copy(
        src_ref=src, dst_ref=dst, send_sem=send, recv_sem=recv, device_id=device, device_id_type=MESH
    )


def drain(ref, sem):
    pltpu.make_async_copy(ref, ref, sem).wait()


def greet(barrier, device):
    pl.semaphore_signal(barrier, inc=1, device_id=device, device_id_type=MESH)


def relay_kernel(
    ids_ref, emb_ref, len_ref, partner_ref, cols_ref, pids_ref,
    pay, hub, stage, got, send1, recv1, gsend, grecv, send2, recv2, asend, arecv,
):
    d, m = lax.axis_index("dom"), lax.axis_index("edge")
    zl, c = m // 2, m % 2
    far, near = (d, (1 - zl) * 2 + c), (d, zl * 2 + 1 - c)
    far_m, near_m = (1 - zl) * 2 + c, zl * 2 + 1 - c
    spoke_m = (d + 3) % 4
    barrier = pltpu.get_barrier_semaphore()

    def hello(j, _):
        greet(barrier, (4 * j + m, spoke_m))
        return 0

    greet(barrier, far)
    greet(barrier, near)
    lax.fori_loop(0, HUBS, hello, 0)

    mine = pl.ds(pl.multiple_of(m * 128, 128), 128)
    pay[0:25] = emb_ref[:, mine].astype(bf16).reshape(25, 16, 128)
    slot = m * 1024 + lax.broadcasted_iota(i32, (8, 128), 0) * 128 + lax.broadcasted_iota(i32, (8, 128), 1)
    for a in range(ID_TILES):
        v = ids_ref[8 * a : 8 * a + 8]
        if a == 0:
            v = jnp.where(slot < len_ref[0], v, 512)
        pay[25 + a] = jnp.concatenate([(v >> 5).astype(f32), (v & 31).astype(f32)], axis=0).astype(bf16)
    pay[30:32] = jnp.zeros((2, 16, 128), bf16)
    pl.semaphore_wait(barrier, HUBS + 2)

    def leg1(i, _):
        remote(pay.at[i], hub.at[d % 4, d // 4], send1, recv1, (4 * i + (m + 1) % 4, d % 4)).start()
        return 0

    lax.fori_loop(0, HUBS, leg1, 0)
    drain(hub.at[m], recv1)
    g_far = remote(hub.at[m], hub.at[m], gsend.at[0], grecv.at[0], far)
    g_near = remote(hub.at[m], hub.at[m], gsend.at[1], grecv.at[1], near)
    g_far.start()
    g_near.start()
    g_far.wait_recv()
    g_fwd = remote(hub.at[far_m], hub.at[far_m], gsend.at[2], grecv.at[2], near)
    g_fwd.start()
    g_near.wait_recv()
    g_fwd.wait_recv()

    def leg2(j, _):
        t = 4 * j + m
        p = partner_ref[t]
        stage[j] = hub[p % 4, p // 4]
        remote(stage.at[j], got.at[d // 4], send2, recv2, (t, spoke_m)).start()
        return 0

    lax.fori_loop(0, HUBS, leg2, 0)
    drain(got, recv2)
    block = got.at[pl.ds(0, 25)]
    a_far = remote(block, cols_ref.at[m], asend.at[0], arecv.at[0], far)
    a_near = remote(block, cols_ref.at[m], asend.at[1], arecv.at[1], near)
    a_far.start()
    a_near.start()
    cols_ref[m] = got[0:25]
    for a in range(ID_TILES):
        v = got[25 + a].astype(f32)
        pids_ref[8 * a : 8 * a + 8] = (v[:8] * 32.0 + v[8:]).astype(i32)
    a_far.wait_recv()
    a_fwd = remote(cols_ref.at[far_m], cols_ref.at[far_m], asend.at[2], arecv.at[2], near)
    a_fwd.start()
    a_near.wait_recv()
    a_fwd.wait_recv()
    for copy in (g_far, g_near, g_fwd, a_far, a_near, a_fwd):
        copy.wait_send()
    drain(pay, send1)
    drain(stage, send2)


def relay(ids, emb, length, partner):
    tile = lambda *lead: pltpu.VMEM((*lead, 16, 128), bf16)
    dma = pltpu.SemaphoreType.DMA
    return pl.pallas_call(
        relay_kernel,
        out_shape=(jax.ShapeDtypeStruct((4, 25, 16, 128), bf16), jax.ShapeDtypeStruct((40, 128), i32)),
        in_specs=[VMEM, VMEM, SMEM, SMEM],
        out_specs=(VMEM, VMEM),
        scratch_shapes=[
            tile(32), tile(4, 32), tile(32), tile(32),
            dma, dma, dma((3,)), dma((3,)), dma, dma, dma((3,)), dma((3,)),
        ],
        compiler_params=pltpu.CompilerParams(
            collective_id=1, has_side_effects=True, vmem_limit_bytes=40 * 2**20
        ),
        name="relay",
    )(ids, emb, length, partner)


def onehots(out, ids, first, rows, lanes):
    for j in range(lanes // 128):
        row = ids[pl.ds(first + j, 1), :]
        hit = lax.broadcasted_iota(i32, (rows, 128), 0) == row
        out[:, 128 * j : 128 * (j + 1)] = jnp.where(hit, 1.0, 0.0).astype(bf16)


def split3(x):
    hi = x.astype(bf16)
    rest = x - hi.astype(f32)
    mid = rest.astype(bf16)
    lo = (rest - mid.astype(f32)).astype(bf16)
    return hi, mid, lo


def dot(a, b, ca=1, cb=0):
    return lax.dot_general(a, b, (((ca,), (cb,)), ((), ())), preferred_element_type=f32)


def add3(x):
    return x[0:400] + x[400:800] + x[800:1200]


def counts(ids, first):
    total = jnp.zeros((512, 128), f32)
    for j in range(8):
        hit = lax.broadcasted_iota(i32, (512, 128), 0) == ids[pl.ds(first + j, 1), :]
        total = total + jnp.where(hit, 1.0, 0.0)
    return dot(jnp.ones((8, 128), bf16), total.astype(bf16), 1, 1)[0:1]


def complex_product(a, b):
    return jnp.concatenate(
        [a[:200] * b[:200] - a[200:] * b[200:], a[:200] * b[200:] + a[200:] * b[:200]], axis=0
    )


def conj_product(a, b):
    return jnp.concatenate(
        [a[:200] * b[:200] + a[200:] * b[200:], a[200:] * b[:200] - a[:200] * b[200:]], axis=0
    )


def compute_kernel(
    emb_ref, cols_ref, rel_ref, ids_ref, pids_ref, grel_ref, grad_ref,
    own_b, other_b, rel3, oh_src, oh_dst, oh_rel, parts, dr3, gt, dnacc,
):
    own_b[...] = emb_ref[...].astype(bf16)
    for m in range(4):
        other_b[:, 128 * m : 128 * (m + 1)] = cols_ref[m].reshape(400, 128)
    hi, mid, lo = split3(rel_ref[...])
    rel3[0:400], rel3[400:800], rel3[800:1200] = hi, mid, lo

    def bucket(ids, h_from, t_from, k, own):
        lanes = pl.ds(pl.multiple_of(k * 512, 512), 512)
        onehots(oh_src.at[:, lanes] if own else oh_src.at[:, pl.ds(0, 512)], ids, 4 * k, 512, 512)
        onehots(oh_dst.at[:, pl.ds(0, 512)] if own else oh_dst.at[:, lanes], ids, 16 + 4 * k, 512, 512)
        onehots(oh_rel.at[:, lanes], ids, 8 + 4 * k, 1024, 512)
        src = oh_src[:, lanes] if own else oh_src[:, 0:512]
        dst = oh_dst[:, 0:512] if own else oh_dst[:, lanes]
        h = dot(h_from[...], src)
        t = dot(t_from[...], dst)
        r = add3(dot(rel3[...], oh_rel[:, lanes]))
        q = complex_product(h, r)
        g_pos = -jax.nn.sigmoid(-jnp.sum(q * t, axis=0, keepdims=True))
        q_b = q.astype(bf16)
        negs = dot(t_from[...], q_b, 0, 0)
        gt[...] = (jax.nn.sigmoid(negs) * 0.03125).astype(bf16)
        return h, t, r, q, q_b, g_pos

    def own_block(k, _):
        lanes = pl.ds(pl.multiple_of(k * 512, 512), 512)
        h, t, r, q, q_b, g_pos = bucket(ids_ref, own_b, other_b, k, True)
        weighted = other_b[...].astype(f32) * counts(ids_ref, 24 + 8 * k)
        w_hi = weighted.astype(bf16)
        w_lo = (weighted - w_hi.astype(f32)).astype(bf16)
        dq = t * g_pos + dot(w_hi, gt[...]) + dot(w_lo, gt[...])
        for i, x in enumerate(split3(conj_product(dq, r))):
            parts[400 * i : 400 * (i + 1), lanes] = x
        for i, x in enumerate(split3(conj_product(dq, h))):
            dr3[400 * i : 400 * (i + 1), lanes] = x
        return 0

    lax.fori_loop(0, 2, own_block, 0)

    def rel_scatter(n, _):
        g = add3(dot(dr3[...], oh_rel[pl.ds(pl.multiple_of(n * 256, 256), 256), :], 1, 1))
        for j in range(2):
            grel_ref[:, 2 * n + j] = g[:, 128 * j : 128 * (j + 1)].reshape(50, 8, 128)
        return 0

    lax.fori_loop(0, 4, rel_scatter, 0)

    def ent_scatter(oh):
        def body(n, _):
            g = add3(dot(parts[...], oh[pl.ds(pl.multiple_of(n * 256, 256), 256), :], 1, 1))
            for j in range(2):
                grad_ref[2 * n + j] = grad_ref[2 * n + j] + g[:, 128 * j : 128 * (j + 1)].reshape(50, 8, 128)
            return 0

        lax.fori_loop(0, 2, body, 0)

    grad_ref[...] = jnp.zeros(grad_ref.shape, f32)
    ent_scatter(oh_src)

    dnacc[...] = jnp.zeros(dnacc.shape, f32)

    def partner_block(k, _):
        lanes = pl.ds(pl.multiple_of(k * 512, 512), 512)
        h, t, r, q, q_b, g_pos = bucket(pids_ref, other_b, own_b, k, False)
        for i, x in enumerate(split3(q * g_pos)):
            parts[400 * i : 400 * (i + 1), lanes] = x
        dnacc[...] = dnacc[...] + dot(q_b, gt[...], 1, 1) * counts(pids_ref, 24 + 8 * k)
        return 0

    lax.fori_loop(0, 2, partner_block, 0)
    ent_scatter(oh_dst)
    for m in range(4):
        grad_ref[m] = grad_ref[m] + dnacc[:, 128 * m : 128 * (m + 1)].reshape(50, 8, 128)


def compute(emb, cols, relations, ids, pids):
    return pl.pallas_call(
        compute_kernel,
        out_shape=(jax.ShapeDtypeStruct((50, 8, 8, 128), f32), jax.ShapeDtypeStruct((4, 50, 8, 128), f32)),
        in_specs=[VMEM] * 5,
        out_specs=(VMEM, VMEM),
        scratch_shapes=[
            pltpu.VMEM((400, 512), bf16), pltpu.VMEM((400, 512), bf16), pltpu.VMEM((1200, 1024), bf16),
            pltpu.VMEM((512, 1024), bf16), pltpu.VMEM((512, 1024), bf16), pltpu.VMEM((1024, 1024), bf16),
            pltpu.VMEM((1200, 1024), bf16), pltpu.VMEM((1200, 1024), bf16),
            pltpu.VMEM((512, 512), bf16), pltpu.VMEM((400, 512), f32),
        ],
        compiler_params=pltpu.CompilerParams(vmem_limit_bytes=56 * 2**20),
        name="bucket_grads",
    )(emb, cols, relations, ids, pids)


def reduce_kernel(
    grel_ref, grad_ref, emb_ref, acc_ref, rel_ref, racc_ref, nemb_ref, nacc_ref, nrel_ref, nracc_ref,
    total, half, in0, a1, in1, b1, in2, c1, in3, y1, a2, jn1, b2, jn2, c2, jn3, x2,
    e0, e1, hsum, nblk, ssem, rsem,
):
    d, m = lax.axis_index("dom"), lax.axis_index("edge")
    zl, c = m // 2, m % 2
    zh, x, y = d // 32, d // 8 % 4, d % 8
    z = zh * 2 + zl
    at = lambda x, y, z: ((z // 2) * 32 + x * 8 + y, (z % 2) * 2 + c)
    near, far = (d, zl * 2 + 1 - c), (d, (1 - zl) * 2 + c)
    xs = [at((x + s) % 4, y, z) for s in range(1, 4)]
    ys = [at(x, (y + s) % 8, z) for s in range(1, 8)]
    zs = [at(x, y, (z + s) % 8) for s in range(1, 8)]
    first = lambda s: at(x, (y + (1 - c) * s) % 8, (z + c * s) % 8)
    last = lambda s: at(x, (y + c * s) % 8, (z + (1 - c) * s) % 8)
    me1 = (1 - c) * y + c * z
    me3 = c * y + (1 - c) * z

    barrier = pltpu.get_barrier_semaphore()
    for device in [near] + xs + ys + zs:
        greet(barrier, device)
    pl.semaphore_wait(barrier, 18)

    sent = []

    def push(src, dst, phase, device):
        copy = remote(src, dst, ssem.at[phase], rsem.at[phase], device)
        copy.start()
        return copy

    other_half, own_half = pl.ds((1 - c) * 200, 200), pl.ds(c * 200, 200)
    push(grel_ref.at[other_half], in0, 0, near)
    for k in range(2):
        push(grad_ref.at[2 * k + 1 - c], e0.at[k], 1, near)

    drain(in0, rsem.at[0])
    a1[...] = grel_ref[pl.ds(c * 200, 100)] + in0[0:100]
    for s in range(1, 4):
        xx = (x + s) % 4
        push(a1.at[pl.ds(25 * xx, 25)], in1.at[x], 2, at(xx, y, z))
    a2[0:100] = grel_ref[pl.ds(c * 200 + 100, 100)] + in0[100:200]
    a2[100:104] = jnp.zeros((4, 8, 128), f32)
    for s in range(1, 8):
        push(a2.at[pl.ds(13 * ((me1 + s) % 8), 13)], jn1.at[me1], 3, first(s))

    drain(e0, rsem.at[1])
    for k in range(2):
        hsum[k] = grad_ref[2 * k + c] + e0[k]
    push(hsum.at[1 - zl], e1, 4, far)

    drain(in1.at[pl.ds(0, 3)], rsem.at[2])
    s1 = a1[pl.ds(25 * x, 25)]
    for s in range(1, 4):
        s1 = s1 + in1[(x + s) % 4]
    b1[0:25] = s1
    b1[25:32] = jnp.zeros((7, 8, 128), f32)
    for s in range(1, 8):
        yy = (y + s) % 8
        push(b1.at[pl.ds(4 * yy, 4)], in2.at[y], 5, at(x, yy, z))

    drain(jn1.at[pl.ds(0, 7)], rsem.at[3])
    s2 = a2[pl.ds(13 * me1, 13)]
    for s in range(1, 8):
        s2 = s2 + jn1[(me1 + s) % 8]
    b2[0:13] = s2
    b2[13:16] = jnp.zeros((3, 8, 128), f32)
    for s in range(1, 4):
        xx = (x + s) % 4
        push(b2.at[pl.ds(4 * xx, 4)], jn2.at[x], 6, at(xx, y, z))

    drain(in2.at[pl.ds(0, 7)], rsem.at[5])
    s1 = b1[pl.ds(4 * y, 4)]
    for s in range(1, 8):
        s1 = s1 + in2[(y + s) % 8]
    c1[...] = s1
    in3[z] = s1
    for s in range(1, 8):
        push(c1, in3.at[z], 7, zs[s - 1])

    drain(jn2.at[pl.ds(0, 3)], rsem.at[6])
    s2 = b2[pl.ds(4 * x, 4)]
    for s in range(1, 4):
        s2 = s2 + jn2[(x + s) % 4]
    c2[...] = s2
    jn3[me3] = s2
    for s in range(1, 8):
        push(c2, jn3.at[me3], 8, last(s))

    drain(e1, rsem.at[4])
    g = hsum[zl] + e1[...]
    mine = pl.ds(pl.multiple_of(m * 128, 128), 128)
    square = jnp.sum(jnp.sum(g * g, axis=0), axis=0, keepdims=True)
    new_acc = acc_ref[:, mine] + square * (1.0 / 400.0)
    step = learn_rate / jnp.sqrt(new_acc)
    nblk[m, 0:50] = emb_ref[:, mine].reshape(50, 8, 128) - g * step
    nblk[m, 50] = jnp.broadcast_to(new_acc, (8, 128))
    push(nblk.at[m], nblk.at[m], 9, far)
    push(nblk.at[m], nblk.at[m], 10, near)

    drain(in3.at[pl.ds(0, 7)], rsem.at[7])
    s1 = in3[0]
    for k in range(1, 8):
        s1 = s1 + in3[k]
    y1[pl.ds(4 * y, 4)] = s1
    for s in range(1, 8):
        push(y1.at[pl.ds(4 * y, 4)], y1.at[pl.ds(4 * y, 4)], 11, ys[s - 1])

    drain(jn3.at[pl.ds(0, 7)], rsem.at[8])
    s2 = jn3[0]
    for k in range(1, 8):
        s2 = s2 + jn3[k]
    x2[pl.ds(4 * x, 4)] = s2
    for s in range(1, 4):
        push(x2.at[pl.ds(4 * x, 4)], x2.at[pl.ds(4 * x, 4)], 12, xs[s - 1])

    far_m, near_m = (1 - zl) * 2 + c, zl * 2 + 1 - c
    drain(nblk.at[m], rsem.at[9])
    push(nblk.at[far_m], nblk.at[far_m], 13, near)

    drain(y1.at[pl.ds(0, 28)], rsem.at[11])
    base = c * 200
    for s in range(1, 4):
        push(y1.at[pl.ds(0, 25)], total.at[pl.ds(base + 25 * x, 25)], 14, xs[s - 1])
    total[pl.ds(base + 25 * x, 25)] = y1[0:25]

    drain(x2.at[pl.ds(0, 12)], rsem.at[12])
    for s in range(1, 8):
        push(x2.at[pl.ds(0, 13)], half.at[pl.ds(13 * me1, 13)], 15, first(s))
    half[pl.ds(13 * me1, 13)] = x2[0:13]

    drain(total.at[pl.ds(0, 75)], rsem.at[14])
    push(total.at[pl.ds(base, 100)], total.at[pl.ds(base, 100)], 16, near)

    drain(half.at[pl.ds(0, 91)], rsem.at[15])
    push(half.at[pl.ds(0, 100)], total.at[pl.ds(base + 100, 100)], 17, near)
    total[pl.ds(base + 100, 100)] = half[0:100]

    drain(nblk.at[m], rsem.at[10])
    drain(nblk.at[m], rsem.at[13])
    for k in range(4):
        nemb_ref[:, 128 * k : 128 * (k + 1)] = nblk[k, 0:50].reshape(400, 128)
        nacc_ref[:, 128 * k : 128 * (k + 1)] = nblk[k, 50, 0:1]

    drain(total.at[pl.ds(0, 100)], rsem.at[16])
    drain(total.at[pl.ds(0, 100)], rsem.at[17])
    for k in range(8):
        lanes = slice(128 * k, 128 * (k + 1))
        rows = [total[8 * i + k] for i in range(50)]
        square = rows[0] * rows[0]
        for v in rows[1:]:
            square = square + v * v
        new_racc = racc_ref[:, lanes] + jnp.sum(square, axis=0, keepdims=True) * (1.0 / 400.0)
        step = learn_rate / jnp.sqrt(new_racc)
        nracc_ref[:, lanes] = new_racc
        for i in range(50):
            nrel_ref[8 * i : 8 * i + 8, lanes] = rel_ref[8 * i : 8 * i + 8, lanes] - rows[i] * step

    drain(in0, ssem.at[0])
    drain(e0, ssem.at[1])
    drain(in1.at[pl.ds(0, 3)], ssem.at[2])
    drain(jn1.at[pl.ds(0, 7)], ssem.at[3])
    drain(e1, ssem.at[4])
    drain(in2.at[pl.ds(0, 7)], ssem.at[5])
    drain(jn2.at[pl.ds(0, 3)], ssem.at[6])
    drain(in3.at[pl.ds(0, 7)], ssem.at[7])
    drain(jn3.at[pl.ds(0, 7)], ssem.at[8])
    for p in (9, 10, 13):
        drain(nblk.at[0], ssem.at[p])
    drain(y1.at[pl.ds(0, 28)], ssem.at[11])
    drain(x2.at[pl.ds(0, 12)], ssem.at[12])
    drain(total.at[pl.ds(0, 75)], ssem.at[14])
    drain(half.at[pl.ds(0, 91)], ssem.at[15])
    drain(total.at[pl.ds(0, 100)], ssem.at[16])
    drain(total.at[pl.ds(0, 100)], ssem.at[17])


def reduce_update(grel, grad, emb, acc, relations, racc):
    t = lambda *lead: pltpu.VMEM((*lead, 8, 128), f32)
    shape = lambda *s: jax.ShapeDtypeStruct(s, f32)
    return pl.pallas_call(
        reduce_kernel,
        out_shape=(shape(400, 512), shape(1, 512), shape(400, 1024), shape(1, 1024)),
        in_specs=[VMEM] * 6,
        out_specs=(VMEM,) * 4,
        scratch_shapes=[
            t(400), t(104), t(200), t(100), t(4, 25), t(32), t(8, 4), t(4), t(8, 4), t(32),
            t(104), t(8, 13), t(16), t(4, 4), t(4), t(8, 4), t(16),
            t(2, 50), t(50), t(2, 50), t(4, 51),
            pltpu.SemaphoreType.DMA((18,)), pltpu.SemaphoreType.DMA((18,)),
        ],
        compiler_params=pltpu.CompilerParams(
            collective_id=2, has_side_effects=True, vmem_limit_bytes=56 * 2**20
        ),
        name="reduce_update",
    )(grel, grad, emb, acc, relations, racc)


def shards(embeddings, accum, relations, rel_accum, src_ids, rel_ids, dst_ids, neg_ids, bucket_len, partner):
    ids = jnp.concatenate([v.reshape(-1, 128) for v in (src_ids, rel_ids, dst_ids, neg_ids)], axis=0)
    position = lax.axis_index("edge") * 1024 + jnp.arange(1024, dtype=i32)
    live_src = jnp.where(position < bucket_len[0], src_ids[0], 512)
    own_ids = jnp.concatenate(
        [v.reshape(-1, 128) for v in (live_src, rel_ids, dst_ids, neg_ids)], axis=0
    )
    cols, pids = relay(ids, embeddings, bucket_len, partner)
    grel, grad = compute(embeddings, cols, relations, own_ids, pids)
    new_emb, new_acc, new_rel, new_racc = reduce_update(
        grel.reshape(400, 8, 128), grad, embeddings, accum.reshape(1, 512), relations, rel_accum.reshape(1, 1024)
    )
    return new_emb, new_acc.reshape(512), new_rel, new_racc.reshape(1024)


def solution(mesh):
    return jax.shard_map(
        shards,
        mesh=mesh,
        in_specs=(
            P(None, "dom"), P("dom"), P(), P(), P("dom", "edge"), P("dom", "edge"), P("dom", "edge"),
            P("dom", "edge", None), P("dom"), P(),
        ),
        out_specs=(P(None, "dom"), P("dom"), P(), P()),
        check_vma=False,
    )
```

time: 551 us -> 131 us (0.24); the launches traced: 542 us -> 130 us
  waiting for transfers between devices: 336 us -> 0 us
  Pallas kernels: 0 us -> 119 us
  local copies, waits for them, and re-layouts: 57.4 us -> 8.4 us
  starting transfers between devices: 44.9 us -> 0 us
  blocking collectives: 34.3 us -> 0 us
  other arithmetic: 34.7 us -> 2.01 us
  matrix products: 18.8 us -> 0 us
  between operations: 15.6 us -> 1.33 us
    psum x2 -> x0, waiting for transfers between devices: 302 us -> none  [the longest x1 256 us: shards(): rel_total = lax.psum(g_rel, ('dom', 'edge'))]
    pallas_call x0 -> x3, Pallas kernels: none -> 119 us  [the longest x1 47.6 us: reduce_update(): pl.pallas_call(reduce_kernel, out_shape=(shape(400, 512), shape(1, 512),...]
    all_to_all x3 -> x0, starting transfers between devices: 44.6 us -> none  [shards(): lax.all_to_all(value, 'dom', split_axis=0, concat_axis=0, tiled=True)]
    all_to_all x1 -> x0, blocking collectives: 34.3 us -> none  [shards(): lax.all_to_all(value, 'dom', split_axis=0, concat_axis=0, tiled=True)]
    all_to_all x3 -> x0, waiting for transfers between devices: 34.3 us -> none  [shards(): lax.all_to_all(value, 'dom', split_axis=0, concat_axis=0, tiled=True)]
    gather x10 -> x0, local copies, waits for them, and re-layouts: 32.4 us -> none  [the longest x2 13.1 us: bucket_terms(): jnp.take(other_b, neg_flat, axis=1).reshape(dim, blocks, negcount)]
    dot_general x6 -> x0, matrix products: 18.8 us -> none  [the longest x3 11.6 us: spread_columns(): jnp.dot(values, onehot, precision=lax.Precision.HIGHEST, preferred_elemen...]
    all_to_all x3 -> x0, other arithmetic: 9.94 us -> none  [shards(): lax.all_to_all(value, 'dom', split_axis=0, concat_axis=0, tiled=True)]
  transfers between devices with their start and end apart: 5 -> 0, of which waited for: 5 -> 0; matrix products, arithmetic and copies ran while one was open for 7% -> 0% of each run, Pallas kernels for 0% -> 0%
where the time goes in v1:
time: 131 us; the launch traced here: 130 us
  Pallas kernels  119 us (91%)
  local copies, waits for them, and re-layouts  8.4 us (6%)
  other arithmetic  2.01 us (2%)
  between operations  1.33 us (1%)
    pallas_call x1, Pallas kernels, reduce_update(): pl.pallas_call(reduce_kernel, out_shape=(shape(400, 512), shape(1, 512),...  47.6 us
    pallas_call x1, Pallas kernels, relay(): pl.pallas_call(relay_kernel, out_shape=(jax.ShapeDtypeStruct((4, 25, 16,...  46 us
    pallas_call x1, Pallas kernels, compute(): pl.pallas_call(compute_kernel, out_shape=(jax.ShapeDtypeStruct((50, 8, 8,...  25.1 us
    unnamed x18, local copies, waits for them, and re-layouts  7.7 us

profile of v1, /device:TPU:1, one launch (start us, length us, event | category | flops | bytes accessed | tf_op | source)
XLA Modules:
  0.0 130.5 jit_solution(10613389209099858003)
XLA Ops:
  1.3 0.7 fusion
  2.0 0.7 reshape.44
  2.7 1.3 %pad_add_fusion.4 = (s32[40,128]{1,0:T(8,128)}, s32[40,128]{1,0:T(8,128)S(1)}) fusion(s32[16,128]{1,0:T(8,128)S(1)} %reshape.44, s32[8,128]{1,0:T(8,128)} %bitcast.13, s32[8,128]{1,0:T(8,128)} %bitcast.14, s32[8,128]{1,0:T(8,128)S(1)} %fusion, s32[8,128]{1,0:T(8,128)} %bitcast.12), kind=kLoop, calls=%fused_computation.4 | loop fusion | flops 30720 | bytes 65536 | tf_op jit(solution)/shard_map/concatenate | solution.py:468
  4.0 0.0 copy-start
  4.0 1.1 copy-done
  5.1 0.0 copy-start.3
  5.1 0.7 copy-done.3
  5.8 46.0 %relay.1 = (bf16[4,25,16,128]{3,2,1,0:T(8,128)(2,1)S(1)}, s32[40,128]{1,0:T(8,128)S(1)}) custom-call(s32[40,128]{1,0:T(8,128)S(1)} %get-tuple-element.21.ids_ref, f32[400,512]{1,0:T(8,128)S(1)} %copy-done, s32[1]{0:T(128)} %copy.18.len_ref, s32[128]{0:T(128)S(1)} %copy-done.3), custom_call_target="tpu_custom_call" | custom-call | tf_op jit(solution)/shard_map/relay/pallas_call | solution.py:112
  51.8 0.0 copy-start.1
  51.8 0.7 copy-done.1
  52.6 0.0 copy-start.2
  52.6 0.6 copy-done.2
  53.2 25.1 %bucket_grads.1 = (f32[50,8,8,128]{3,2,1,0:T(8,128)}, f32[4,50,8,128]{3,2,1,0:T(8,128)}) custom-call(f32[400,512]{1,0:T(8,128)} %emb_ref.5, bf16[4,25,16,128]{3,2,1,0:T(8,128)(2,1)} %copy-done.1, f32[400,1024]{1,0:T(8,128)} %rel_ref.3, s32[40,128]{1,0:T(8,128)} %get-tuple-element.20.ids_ref, s32[40,128]{1,0:T(8,128)} %copy-done.2), custom_call_target="tpu_custom_call" | custom-call | tf_op jit(solution)/shard_map/bucket_grads/pallas_call | solution.py:250
  78.3 47.6 %reduce_update.1 = (f32[400,512]{1,0:T(8,128)}, f32[1,512]{1,0:T(1,128)}, f32[400,1024]{1,0:T(8,128)}, f32[1,1024]{1,0:T(1,128)}) custom-call(f32[400,8,128]{2,1,0:T(8,128)} %bitcast.10, f32[4,50,8,128]{3,2,1,0:T(8,128)} %get-tuple-element.15.grad_ref, f32[400,512]{1,0:T(8,128)} %emb_ref.5, f32[1,512]{1,0:T(1,128)} %bitcast.17, f32[400,1024]{1,0:T(8,128)} %rel_ref.3, ...), custom_call_target="tpu_custom_call" | custom-call | tf_op jit(solution)/shard_map/reduce_update/pallas_call | solution.py:446
  125.9 0.0 copy-start.6
  125.9 0.0 copy-start.4
  125.9 2.2 %copy.19 = f32[400,512]{1,0:T(8,128)} copy(f32[400,512]{1,0:T(8,128)} %get-tuple-element.26) | data formatting | bytes 1638400
  128.1 0.0 copy-done.6
  128.1 0.6 copy.20
  128.7 0.0 copy-done.4
  128.7 0.0 copy-start.5
  128.7 1.2 copy.21
  129.9 0.0 copy-done.5
  129.9 0.6 copy.22
Async XLA Ops:
  4.0 1.1 copy-start
  5.1 0.7 copy-start.3
  51.8 0.7 copy-start.1
  52.6 0.6 copy-start.2
  125.9 2.2 %copy-start.6 = (f32[1,512]{1,0:T(1,128)S(1)}, f32[1,512]{1,0:T(1,128)}, u32[]{:S(2)}) copy-start(f32[1,512]{1,0:T(1,128)} %get-tuple-element.17) | copy-start | bytes 6148
  125.9 2.8 %copy-start.4 = (f32[400,1024]{1,0:T(8,128)S(1)}, f32[400,1024]{1,0:T(8,128)}, u32[]{:S(2)}) copy-start(f32[400,1024]{1,0:T(8,128)} %get-tuple-element.28) | copy-start | bytes 4915204
  128.7 1.2 copy-start.5

commit v2 on v0

v2 whole, which is shorter than its diff:
```python
import jax
import jax.numpy as jnp
from jax import lax
from jax.experimental import pallas as pl
from jax.experimental.pallas import tpu as pltpu
from jax.sharding import PartitionSpec as P

MESH = pl.DeviceIdType.MESH
VMEM = pl.BlockSpec(memory_space=pltpu.VMEM)
SMEM = pl.BlockSpec(memory_space=pltpu.SMEM)
ANY = pl.BlockSpec(memory_space=pl.ANY)
f32, bf16, i32 = jnp.float32, jnp.bfloat16, jnp.int32
learn_rate = 0.1
HUBS = 32
ID_TILES = 5
SIZE = {"x": 4, "y": 8, "z": 8, "u": 8, "v": 8}
STREAMS = ((0, 4, "uxv"), (4, 2, "xyz"), (6, 2, "xzy"))


def remote(src, dst, send, recv, device):
    return pltpu.make_async_remote_copy(
        src_ref=src, dst_ref=dst, send_sem=send, recv_sem=recv, device_id=device, device_id_type=MESH
    )


def drain(ref, sem):
    pltpu.make_async_copy(ref, ref, sem).wait()


def levels(count, axes):
    n1 = -(-count // SIZE[axes[0]])
    return n1, -(-n1 // SIZE[axes[1]])


def stream_scratch(count, axes):
    n1, n2 = levels(count, axes)
    na, nb, nc = (SIZE[a] for a in axes)
    t = lambda *lead: pltpu.VMEM((*lead, 8, 128), f32)
    return [t(count), t(na * n1), t(na, n1), t(nb * n2), t(nb, n2), t(n2), t(nc, n2), t(nb * n2), t(na * n1)]


def onehots(out, ids, first, rows):
    for j in range(4):
        hit = lax.broadcasted_iota(i32, (rows, 128), 0) == ids[first + j : first + j + 1, :]
        out[:, 128 * j : 128 * (j + 1)] = jnp.where(hit, 1.0, 0.0).astype(bf16)


def split3(x):
    hi = x.astype(bf16)
    rest = x - hi.astype(f32)
    mid = rest.astype(bf16)
    lo = (rest - mid.astype(f32)).astype(bf16)
    return hi, mid, lo


def dot(a, b, ca=1, cb=0):
    return lax.dot_general(a, b, (((ca,), (cb,)), ((), ())), preferred_element_type=f32)


def add3(x):
    return x[0:400] + x[400:800] + x[800:1200]


def counts(ids, first):
    total = jnp.zeros((512, 128), f32)
    for j in range(8):
        hit = lax.broadcasted_iota(i32, (512, 128), 0) == ids[first + j : first + j + 1, :]
        total = total + jnp.where(hit, 1.0, 0.0)
    return dot(jnp.ones((8, 128), bf16), total.astype(bf16), 1, 1)[0:1]


def complex_product(a, b):
    return jnp.concatenate(
        [a[:200] * b[:200] - a[200:] * b[200:], a[:200] * b[200:] + a[200:] * b[:200]], axis=0
    )


def conj_product(a, b):
    return jnp.concatenate(
        [a[:200] * b[:200] + a[200:] * b[200:], a[200:] * b[:200] - a[:200] * b[200:]], axis=0
    )


def round_kernel(*refs):
    refs = list(refs)
    take = lambda n: [refs.pop(0) for _ in range(n)]
    src_in, rel_in, dst_in, neg_in, emb_in, acc_in, relations_in, len_ref, partner_ref = take(9)
    total, nblk = take(2)
    src_v, rel_v, dst_v, neg_v, emb, acc, relations, in_sem = take(8)
    pay, hub, stage, got, cols, send1, recv1, gsend, grecv, send2, recv2, asend, arecv = take(13)
    ids, pids, own_b, other_b, rel3, oh_src, oh_dst, oh_rel, p_src, p_dst, p_rel = take(11)
    h_s, r_s, q_s, dq_s, pr_s, dr3, parts, gt, dn, grel, grad = take(11)
    e0, e1, hsum, esend, erecv, ssem, rsem = take(7)
    streams = [(axes, 25 * n, 25 * lane, take(9)) for lane, n, axes in STREAMS]

    d, m = lax.axis_index("dom"), lax.axis_index("edge")
    zl, c = m // 2, m % 2
    zh, x, y = d // 32, d // 8 % 4, d % 8
    z = zh * 2 + zl
    at = lambda x, y, z: ((z // 2) * 32 + x * 8 + y, (z % 2) * 2 + c)
    far_m, near_m = (1 - zl) * 2 + c, zl * 2 + 1 - c
    far, near = (d, far_m), (d, near_m)
    spoke_m = (d + 3) % 4
    mine = pl.ds(pl.multiple_of(m * 128, 128), 128)
    place = {"x": x, "y": y, "z": z, "u": (1 - c) * y + c * z, "v": c * y + (1 - c) * z}
    peer = {
        "x": lambda s: at((x + s) % 4, y, z),
        "y": lambda s: at(x, (y + s) % 8, z),
        "z": lambda s: at(x, y, (z + s) % 8),
        "u": lambda s: at(x, (y + (1 - c) * s) % 8, (z + c * s) % 8),
        "v": lambda s: at(x, (y + c * s) % 8, (z + (1 - c) * s) % 8),
    }

    barrier = pltpu.get_barrier_semaphore()
    greet = lambda device: pl.semaphore_signal(barrier, inc=1, device_id=device, device_id_type=MESH)
    inputs = [
        pltpu.make_async_copy(a, b, in_sem.at[i])
        for i, (a, b) in enumerate(
            [(src_in, src_v), (rel_in, rel_v), (dst_in, dst_v), (neg_in, neg_v), (emb_in, emb), (acc_in, acc),
             (relations_in, relations)]
        )
    ]
    for copy in inputs:
        copy.start()

    def hello(j, _):
        greet((4 * j + m, spoke_m))
        return 0

    lax.fori_loop(0, HUBS, hello, 0)
    greet(near)
    for axis in "xyz":
        for s in range(1, SIZE[axis]):
            greet(peer[axis](s))

    for copy in inputs[:5]:
        copy.wait()
    pay[0:25] = emb[:, mine].astype(bf16).reshape(25, 16, 128)
    slot = m * 1024 + lax.broadcasted_iota(i32, (8, 128), 0) * 128 + lax.broadcasted_iota(i32, (8, 128), 1)
    rows = [src_v, rel_v, dst_v, neg_v.at[0, 0:1], neg_v.at[0, 1:2]]
    for a, row in enumerate(rows):
        for j in range(8):
            ids[8 * a + j : 8 * a + j + 1, :] = row[0:1, 128 * j : 128 * (j + 1)]
        v = ids[8 * a : 8 * a + 8, :]
        if a == 0:
            v = jnp.where(slot < len_ref[0], v, 512)
            ids[0:8, :] = v
        pay[25 + a] = jnp.concatenate([(v >> 5).astype(f32), (v & 31).astype(f32)], axis=0).astype(bf16)
    pay[30:32] = jnp.zeros((2, 16, 128), bf16)
    pl.semaphore_wait(barrier, HUBS + 18)

    def leg1(i, _):
        remote(pay.at[i], hub.at[d % 4, d // 4], send1, recv1, (4 * i + (m + 1) % 4, d % 4)).start()
        return 0

    lax.fori_loop(0, HUBS, leg1, 0)

    lanes = [slice(0, 512), slice(512, 1024)]

    def gather_rel(hot, ids, k, out):
        onehots(hot, ids, 8 + 4 * k, 1024)
        out[:, lanes[k]] = add3(dot(rel3[...], hot[...]))

    def own_start(k):
        onehots(oh_src.at[:, lanes[k]], ids, 4 * k, 512)
        h = dot(own_b[...], oh_src[:, lanes[k]])
        h_s[:, lanes[k]] = h
        q_s[:, lanes[k]] = complex_product(h, r_s[:, lanes[k]])
        onehots(oh_dst.at[:, lanes[k]], ids, 16 + 4 * k, 512)

    own_b[...] = emb[...].astype(bf16)
    inputs[6].wait()
    rel3[0:400], rel3[400:800], rel3[800:1200] = split3(relations[...])
    gather_rel(oh_rel.at[:, lanes[0]], ids, 0, r_s)

    drain(hub.at[m], recv1)
    g_far = remote(hub.at[m], hub.at[m], gsend.at[0], grecv.at[0], far)
    g_near = remote(hub.at[m], hub.at[m], gsend.at[1], grecv.at[1], near)
    g_far.start()
    g_near.start()
    gather_rel(oh_rel.at[:, lanes[1]], ids, 1, r_s)
    g_far.wait_recv()
    g_fwd = remote(hub.at[far_m], hub.at[far_m], gsend.at[2], grecv.at[2], near)
    g_fwd.start()
    g_near.wait_recv()
    g_fwd.wait_recv()

    def leg2(j, _):
        t = 4 * j + m
        p = partner_ref[t]
        stage[j] = hub[p % 4, p // 4]
        remote(stage.at[j], got.at[d // 4], send2, recv2, (t, spoke_m)).start()
        return 0

    lax.fori_loop(0, HUBS, leg2, 0)
    own_start(0)
    own_start(1)
    count = [counts(ids, 24 + 8 * k) for k in range(2)]
    drain(got, recv2)

    block = got.at[pl.ds(0, 25)]
    a_far = remote(block, cols.at[m], asend.at[0], arecv.at[0], far)
    a_near = remote(block, cols.at[m], asend.at[1], arecv.at[1], near)
    a_far.start()
    a_near.start()
    cols[m] = got[0:25]
    for a in range(ID_TILES):
        v = got[25 + a].astype(f32)
        pids[8 * a : 8 * a + 8, :] = (v[:8] * 32.0 + v[8:]).astype(i32)
    gather_rel(p_rel, pids, 0, pr_s)
    a_far.wait_recv()
    a_fwd = remote(cols.at[far_m], cols.at[far_m], asend.at[2], arecv.at[2], near)
    a_fwd.start()
    gather_rel(p_rel, pids, 1, pr_s)
    a_near.wait_recv()
    a_fwd.wait_recv()
    for k in range(4):
        other_b[:, 128 * k : 128 * (k + 1)] = cols[k].reshape(400, 128)

    for k in range(2):
        q = q_s[:, lanes[k]]
        t = dot(other_b[...], oh_dst[:, lanes[k]])
        g_pos = -jax.nn.sigmoid(-jnp.sum(q * t, axis=0, keepdims=True))
        negs = dot(other_b[...], q.astype(bf16), 0, 0)
        gt[...] = (jax.nn.sigmoid(negs) * 0.03125).astype(bf16)
        weighted = other_b[...].astype(f32) * count[k]
        w_hi = weighted.astype(bf16)
        w_lo = (weighted - w_hi.astype(f32)).astype(bf16)
        dq = t * g_pos + dot(w_hi, gt[...]) + dot(w_lo, gt[...])
        dq_s[:, lanes[k]] = dq
        for i, v in enumerate(split3(conj_product(dq, h_s[:, lanes[k]]))):
            dr3[400 * i : 400 * (i + 1), lanes[k]] = v

    def rel_scatter(n):
        g = add3(dot(dr3[...], oh_rel[256 * n : 256 * (n + 1), :], 1, 1))
        for j in range(2):
            for half in range(2):
                grel[half, pl.ds(25 * (2 * n + j), 25)] = g[
                    200 * half : 200 * (half + 1), 128 * j : 128 * (j + 1)
                ].reshape(25, 8, 128)

    def step(i, level):
        axes, T, base, (in0, a, in1, b, in2, last, in3, gb, ga) = streams[i]
        n1, n2 = levels(T, axes)
        (A, B, C), (na, nb, nc) = axes, [SIZE[k] for k in axes]
        ma, mb, mc = place[A], place[B], place[C]
        zeros = lambda n: jnp.zeros((n, 8, 128), f32)

        def push(src, dst, device):
            remote(src, dst, ssem.at[i, level], rsem.at[i, level], device).start()

        if level == 0:
            push(grel.at[1 - c, pl.ds(base, T)], in0, near)
        elif level == 1:
            drain(in0, rsem.at[i, 0])
            a[0:T] = grel[c, pl.ds(base, T)] + in0[...]
            if na * n1 > T:
                a[T : na * n1] = zeros(na * n1 - T)
            for s in range(1, na):
                push(a.at[pl.ds(n1 * ((ma + s) % na), n1)], in1.at[ma], peer[A](s))
        elif level == 2:
            drain(in1.at[pl.ds(0, na - 1)], rsem.at[i, 1])
            v = a[pl.ds(n1 * ma, n1)]
            for s in range(1, na):
                v = v + in1[(ma + s) % na]
            b[0:n1] = v
            if nb * n2 > n1:
                b[n1 : nb * n2] = zeros(nb * n2 - n1)
            for s in range(1, nb):
                push(b.at[pl.ds(n2 * ((mb + s) % nb), n2)], in2.at[mb], peer[B](s))
        elif level == 3:
            drain(in2.at[pl.ds(0, nb - 1)], rsem.at[i, 2])
            v = b[pl.ds(n2 * mb, n2)]
            for s in range(1, nb):
                v = v + in2[(mb + s) % nb]
            last[...] = v
            in3[mc] = v
            for s in range(1, nc):
                push(last, in3.at[mc], peer[C](s))
        elif level == 4:
            drain(in3.at[pl.ds(0, nc - 1)], rsem.at[i, 3])
            v = in3[0]
            for s in range(1, nc):
                v = v + in3[s]
            spot = pl.ds(n2 * mb, n2)
            gb[spot] = v
            for s in range(1, nb):
                push(gb.at[spot], gb.at[spot], peer[B](s))
        elif level == 5:
            drain(gb.at[pl.ds(0, (nb - 1) * n2)], rsem.at[i, 4])
            spot = pl.ds(n1 * ma, n1)
            for s in range(1, na):
                push(gb.at[pl.ds(0, n1)], ga.at[spot], peer[A](s))
            ga[spot] = gb[0:n1]
        elif level == 6:
            drain(ga.at[pl.ds(0, (na - 1) * n1)], rsem.at[i, 5])
            push(ga.at[pl.ds(0, T)], total.at[c, pl.ds(base, T)], near)
            total[c, pl.ds(base, T)] = ga[0:T]
        else:
            drain(in0, rsem.at[i, 6])
            drain(in0, ssem.at[i, 0])
            drain(in1.at[pl.ds(0, na - 1)], ssem.at[i, 1])
            drain(in2.at[pl.ds(0, nb - 1)], ssem.at[i, 2])
            drain(in3.at[pl.ds(0, nc - 1)], ssem.at[i, 3])
            drain(gb.at[pl.ds(0, (nb - 1) * n2)], ssem.at[i, 4])
            drain(ga.at[pl.ds(0, (na - 1) * n1)], ssem.at[i, 5])
            drain(in0, ssem.at[i, 6])

    held = {}

    def partner_a(k):
        onehots(p_src, pids, 4 * k, 512)
        onehots(p_dst.at[:, lanes[k]], pids, 16 + 4 * k, 512)
        h = dot(other_b[...], p_src[...])
        t = dot(own_b[...], p_dst[:, lanes[k]])
        q = complex_product(h, pr_s[:, lanes[k]])
        q_s[:, lanes[k]] = q
        g_pos = -jax.nn.sigmoid(-jnp.sum(q * t, axis=0, keepdims=True))
        for i, v in enumerate(split3(q * g_pos)):
            parts[400 * i : 400 * (i + 1), lanes[k]] = v

    def partner_b(k):
        q_b = q_s[:, lanes[k]].astype(bf16)
        gt[...] = (jax.nn.sigmoid(dot(own_b[...], q_b, 0, 0)) * 0.03125).astype(bf16)
        v = dot(q_b, gt[...], 1, 1) * counts(pids, 24 + 8 * k)
        dn[...] = v if k == 0 else dn[...] + v

    def dh(k):
        for i, v in enumerate(split3(conj_product(dq_s[:, lanes[k]], r_s[:, lanes[k]]))):
            dr3[400 * i : 400 * (i + 1), lanes[k]] = v

    def ent_scatter(n):
        rows = slice(256 * n, 256 * (n + 1))
        g = add3(dot(dr3[...], oh_src[rows, :], 1, 1) + dot(parts[...], p_dst[rows, :], 1, 1)) + dn[:, rows]
        for j in range(2):
            grad[2 * n + j] = g[:, 128 * j : 128 * (j + 1)].reshape(50, 8, 128)

    def ent(level):
        def push(src, dst, device):
            remote(src, dst, esend.at[level], erecv.at[level], device).start()

        if level == 0:
            for k in range(2):
                push(grad.at[2 * k + 1 - c], e0.at[k], near)
        elif level == 1:
            drain(e0, erecv.at[0])
            for k in range(2):
                hsum[k] = grad[2 * k + c] + e0[k]
            push(hsum.at[1 - zl], e1, far)
        elif level == 2:
            drain(e1, erecv.at[1])
            g = hsum[zl] + e1[...]
            square = jnp.sum(jnp.sum(g * g, axis=0), axis=0, keepdims=True)
            new_acc = acc[:, mine] + square * (1.0 / 400.0)
            nblk[m, 0:50] = emb[:, mine].reshape(50, 8, 128) - g * (learn_rate / jnp.sqrt(new_acc))
            nblk[m, 50] = jnp.broadcast_to(new_acc, (8, 128))
            push(nblk.at[m], nblk.at[m], far)
        elif level == 3:
            push(nblk.at[m], nblk.at[m], near)
        elif level == 4:
            drain(nblk.at[m], erecv.at[2])
            push(nblk.at[far_m], nblk.at[far_m], near)
        else:
            drain(nblk.at[m], erecv.at[3])
            drain(nblk.at[m], erecv.at[4])
            drain(e0, esend.at[0])
            drain(e1, esend.at[1])
            for k in range(2, 5):
                drain(nblk.at[m], esend.at[k])

    rel_scatter(0)
    rel_scatter(1)
    step(0, 0)
    rel_scatter(2)
    step(1, 0)
    step(0, 1)
    rel_scatter(3)
    step(2, 0)
    step(1, 1)
    step(2, 1)
    inputs[5].wait()
    dh(0)
    dh(1)
    partner_a(0)
    step(1, 2)
    partner_b(0)
    step(2, 2)
    step(0, 2)
    partner_a(1)
    step(1, 3)
    step(0, 3)
    step(2, 3)
    partner_b(1)
    ent_scatter(0)
    step(1, 4)
    step(0, 4)
    ent_scatter(1)
    ent(0)
    step(2, 4)
    step(1, 5)
    step(0, 5)
    ent(1)
    step(2, 5)
    step(1, 6)
    step(0, 6)
    ent(2)
    ent(3)
    step(2, 6)
    ent(4)
    ent(5)
    for i in range(3):
        step(i, 7)

    for copy in (g_far, g_near, g_fwd, a_far, a_near, a_fwd):
        copy.wait_send()
    drain(pay, send1)
    drain(stage, send2)


def bucket_round(*args):
    tile = lambda *lead: pltpu.VMEM((*lead, 16, 128), bf16)
    t = lambda *lead: pltpu.VMEM((*lead, 8, 128), f32)
    V = pltpu.VMEM
    dma = pltpu.SemaphoreType.DMA
    scratch = [
        V((1, 1024), i32), V((1, 1024), i32), V((1, 1024), i32), V((1, 2, 1024), i32), V((400, 512), f32),
        V((1, 512), f32), V((400, 1024), f32), dma((7,)),
        tile(32), tile(4, 32), tile(32), tile(32), tile(4, 25),
        dma, dma, dma((3,)), dma((3,)), dma, dma, dma((3,)), dma((3,)),
        V((40, 128), i32), V((40, 128), i32), V((400, 512), bf16), V((400, 512), bf16), V((1200, 1024), bf16),
        V((512, 1024), bf16), V((512, 1024), bf16), V((1024, 1024), bf16),
        V((512, 512), bf16), V((512, 1024), bf16), V((1024, 512), bf16),
        V((400, 1024), f32), V((400, 1024), f32), V((400, 1024), f32), V((400, 1024), f32), V((400, 1024), f32),
        V((1200, 1024), bf16), V((1200, 1024), bf16), V((512, 512), bf16), V((400, 512), f32),
        t(2, 200), t(4, 50),
        t(2, 50), t(50), t(2, 50), dma((5,)), dma((5,)), dma((3, 7)), dma((3, 7)),
    ]
    for _, n, axes in STREAMS:
        scratch += stream_scratch(25 * n, axes)
    return pl.pallas_call(
        round_kernel,
        out_shape=(jax.ShapeDtypeStruct((2, 200, 8, 128), f32), jax.ShapeDtypeStruct((4, 51, 8, 128), f32)),
        in_specs=[ANY] * 7 + [SMEM] * 2,
        out_specs=(VMEM, VMEM),
        scratch_shapes=scratch,
        compiler_params=pltpu.CompilerParams(
            collective_id=1, has_side_effects=True, vmem_limit_bytes=56 * 2**20
        ),
        name="bucket_round",
    )(*args)


def update_kernel(total, nblk, rel_ref, racc_ref, nemb_ref, nacc_ref, nrel_ref, nracc_ref):
    for k in range(8):
        lanes = slice(128 * k, 128 * (k + 1))
        square = jnp.zeros((8, 128), f32)
        for half in range(2):
            for i in range(25):
                v = total[half, 25 * k + i]
                square = square + v * v
        new_racc = racc_ref[:, lanes] + jnp.sum(square, axis=0, keepdims=True) * (1.0 / 400.0)
        rate = learn_rate / jnp.sqrt(new_racc)
        nracc_ref[:, lanes] = new_racc
        for half in range(2):
            rows = slice(200 * half, 200 * (half + 1))
            g = total[half, 25 * k : 25 * (k + 1)].reshape(200, 128)
            nrel_ref[rows, lanes] = rel_ref[rows, lanes] - g * rate
    for k in range(4):
        lanes = slice(128 * k, 128 * (k + 1))
        nemb_ref[:, lanes] = nblk[k, 0:50].reshape(400, 128)
        nacc_ref[:, lanes] = nblk[k, 50, 0:1]


def update(total, nblk, relations, racc):
    shape = lambda *s: jax.ShapeDtypeStruct(s, f32)
    return pl.pallas_call(
        update_kernel,
        out_shape=(shape(400, 512), shape(1, 512), shape(400, 1024), shape(1, 1024)),
        in_specs=[VMEM] * 4,
        out_specs=(VMEM,) * 4,
        compiler_params=pltpu.CompilerParams(vmem_limit_bytes=32 * 2**20),
        name="update",
    )(total, nblk, relations, racc)


def shards(embeddings, accum, relations, rel_accum, src_ids, rel_ids, dst_ids, neg_ids, bucket_len, partner):
    total, nblk = bucket_round(
        src_ids, rel_ids, dst_ids, neg_ids, embeddings, accum.reshape(1, 512), relations, bucket_len, partner
    )
    new_emb, new_acc, new_rel, new_racc = update(total, nblk, relations, rel_accum.reshape(1, 1024))
    return new_emb, new_acc.reshape(512), new_rel, new_racc.reshape(1024)


def solution(mesh):
    return jax.shard_map(
        shards,
        mesh=mesh,
        in_specs=(
            P(None, "dom"), P("dom"), P(), P(), P("dom", "edge"), P("dom", "edge"), P("dom", "edge"),
            P("dom", "edge", None), P("dom"), P(),
        ),
        out_specs=(P(None, "dom"), P("dom"), P(), P()),
        check_vma=False,
    )
```

time: 551 us -> 101 us (0.18); the launches traced: 542 us -> 100 us
  waiting for transfers between devices: 336 us -> 0 us
  Pallas kernels: 0 us -> 96.4 us
  local copies, waits for them, and re-layouts: 57.4 us -> 2.58 us
  starting transfers between devices: 44.9 us -> 0 us
  other arithmetic: 34.7 us -> 0 us
  blocking collectives: 34.3 us -> 0 us
  matrix products: 18.8 us -> 0 us
  between operations: 15.6 us -> 1.45 us
    psum x2 -> x0, waiting for transfers between devices: 302 us -> none  [the longest x1 256 us: shards(): rel_total = lax.psum(g_rel, ('dom', 'edge'))]
    pallas_call x0 -> x2, Pallas kernels: none -> 96.4 us  [the longest x1 94.5 us: bucket_round(): pl.pallas_call(round_kernel, out_shape=(jax.ShapeDtypeStruct((2, 200, 8,...]
    all_to_all x3 -> x0, starting transfers between devices: 44.6 us -> none  [shards(): lax.all_to_all(value, 'dom', split_axis=0, concat_axis=0, tiled=True)]
    all_to_all x1 -> x0, blocking collectives: 34.3 us -> none  [shards(): lax.all_to_all(value, 'dom', split_axis=0, concat_axis=0, tiled=True)]
    all_to_all x3 -> x0, waiting for transfers between devices: 34.3 us -> none  [shards(): lax.all_to_all(value, 'dom', split_axis=0, concat_axis=0, tiled=True)]
    gather x10 -> x0, local copies, waits for them, and re-layouts: 32.4 us -> none  [the longest x2 13.1 us: bucket_terms(): jnp.take(other_b, neg_flat, axis=1).reshape(dim, blocks, negcount)]
    dot_general x6 -> x0, matrix products: 18.8 us -> none  [the longest x3 11.6 us: spread_columns(): jnp.dot(values, onehot, precision=lax.Precision.HIGHEST, preferred_elemen...]
    unnamed x42 -> x8, local copies, waits for them, and re-layouts: 12.7 us -> 2.58 us
  transfers between devices with their start and end apart: 5 -> 0, of which waited for: 5 -> 0; matrix products, arithmetic and copies ran while one was open for 7% -> 0% of each run, Pallas kernels for 0% -> 0%
where the time goes in v2:
time: 101 us; the launch traced here: 100 us
  Pallas kernels  96.4 us (95%)
  local copies, waits for them, and re-layouts  2.58 us (3%)
  between operations  1.45 us (1%)
    pallas_call x1, Pallas kernels, bucket_round(): pl.pallas_call(round_kernel, out_shape=(jax.ShapeDtypeStruct((2, 200, 8,...  94.5 us
    unnamed x8, local copies, waits for them, and re-layouts  2.58 us

profile of v2, /device:TPU:1, one launch (start us, length us, event | category | flops | bytes accessed | tf_op | source)
XLA Modules:
  0.0 100.4 jit_solution(906874720375614650)
XLA Ops:
  0.6 0.0 copy-start
  0.6 0.0 copy-start.3
  1.4 94.5 %bucket_round.1 = (f32[2,200,8,128]{3,2,1,0:T(8,128)}, f32[4,51,8,128]{3,2,1,0:T(8,128)}) custom-call(s32[1,1024]{1,0:T(1,128)} %refs_0_.1, s32[1,1024]{1,0:T(1,128)} %refs_1_.1, s32[1,1024]{1,0:T(1,128)} %refs_2_.1, s32[1,2,1024]{2,1,0:T(2,128)} %refs_3_.1, f32[400,512]{1,0:T(8,128)} %refs_4_.1, f32[1,512]{1,0:T(1,128)} %bitcast.5, f32[400,1024]{1,0:T(8,128)} %rel_ref.1, ...), custom_call_target="tpu_custom_call" | custom-call | tf_op jit(solution)/shard_map/bucket_round/pallas_call | solution.py:440
  95.9 0.0 copy-done
  95.9 0.0 copy-done.3
  95.9 0.0 copy-start.1
  95.9 1.4 %copy-done.1 = f32[2,200,8,128]{3,2,1,0:T(8,128)S(1)} copy-done((f32[2,200,8,128]{3,2,1,0:T(8,128)S(1)}, f32[2,200,8,128]{3,2,1,0:T(8,128)}, u32[]{:S(2)}) %copy-start.1) | copy-done | bytes 1638424
  97.3 0.0 copy-start.2
  97.3 1.1 %copy-done.2 = f32[4,51,8,128]{3,2,1,0:T(8,128)S(1)} copy-done((f32[4,51,8,128]{3,2,1,0:T(8,128)S(1)}, f32[4,51,8,128]{3,2,1,0:T(8,128)}, u32[]{:S(2)}) %copy-start.2) | copy-done | bytes 835608
  98.5 1.9 %update.1 = (f32[400,512]{1,0:T(8,128)}, f32[1,512]{1,0:T(1,128)}, f32[400,1024]{1,0:T(8,128)}, f32[1,1024]{1,0:T(1,128)}) custom-call(f32[2,200,8,128]{3,2,1,0:T(8,128)S(1)} %copy-done.1, f32[4,51,8,128]{3,2,1,0:T(8,128)S(1)} %copy-done.2, f32[400,1024]{1,0:T(8,128)S(1)} %copy-done, f32[1,1024]{1,0:T(1,128)S(1)} %bitcast.4), custom_call_target="tpu_custom_call" | custom-call | tf_op jit(solution)/shard_map/update/pallas_call | solution.py:476
Async XLA Ops:
  0.6 95.3 %copy-start = (f32[400,1024]{1,0:T(8,128)S(1)}, f32[400,1024]{1,0:T(8,128)}, u32[]{:S(2)}) copy-start(f32[400,1024]{1,0:T(8,128)} %rel_ref.1) | copy-start | bytes 4915204
  0.6 95.3 %copy-start.3 = (f32[1024]{0:T(1024)S(1)}, f32[1024]{0:T(1024)}, u32[]{:S(2)}) copy-start(f32[1024]{0:T(1024)} %param.13) | copy-start | bytes 12292
  95.9 1.4 %copy-start.1 = (f32[2,200,8,128]{3,2,1,0:T(8,128)S(1)}, f32[2,200,8,128]{3,2,1,0:T(8,128)}, u32[]{:S(2)}) copy-start(f32[2,200,8,128]{3,2,1,0:T(8,128)} %get-tuple-element.10.total) | copy-start | bytes 4915204
  97.3 1.1 %copy-start.2 = (f32[4,51,8,128]{3,2,1,0:T(8,128)S(1)}, f32[4,51,8,128]{3,2,1,0:T(8,128)}, u32[]{:S(2)}) copy-start(f32[4,51,8,128]{3,2,1,0:T(8,128)} %get-tuple-element.11.nblk) | copy-start | bytes 2506756

commit v3 on v2

--- a/solution.py
+++ b/solution.py
@@ -14,7 +14,7 @@
 HUBS = 32
 ID_TILES = 5
 SIZE = {"x": 4, "y": 8, "z": 8, "u": 8, "v": 8}
-STREAMS = ((0, 4, "uxv"), (4, 2, "xyz"), (6, 2, "xzy"))
+STREAMS = ((0, 2, "uxv"), (2, 2, "vxu"), (4, 2, "xyz"), (6, 2, "xzy"))
 
 
 def remote(src, dst, send, recv, device):
@@ -85,12 +85,12 @@
     refs = list(refs)
     take = lambda n: [refs.pop(0) for _ in range(n)]
     src_in, rel_in, dst_in, neg_in, emb_in, acc_in, relations_in, len_ref, partner_ref = take(9)
-    total, nblk = take(2)
+    total, nemb_out, nacc_out = take(3)
     src_v, rel_v, dst_v, neg_v, emb, acc, relations, in_sem = take(8)
-    pay, hub, stage, got, cols, send1, recv1, gsend, grecv, send2, recv2, asend, arecv = take(13)
+    pay, hub, stage, got, cols, nblk, send1, recv1, gsend, grecv, send2, recv2, asend, arecv = take(14)
     ids, pids, own_b, other_b, rel3, oh_src, oh_dst, oh_rel, p_src, p_dst, p_rel = take(11)
-    h_s, r_s, q_s, dq_s, pr_s, dr3, parts, gt, dn, grel, grad = take(11)
-    e0, e1, hsum, esend, erecv, ssem, rsem = take(7)
+    h_s, r_s, q_s, qb_s, t_s, dq_s, pr_s, cnt, dr3, parts, gt, dn, grel, grad = take(14)
+    e0, e1, hsum, esend, erecv, ssem, rsem, osem = take(8)
     streams = [(axes, 25 * n, 25 * lane, take(9)) for lane, n, axes in STREAMS]
 
     d, m = lax.axis_index("dom"), lax.axis_index("edge")
@@ -101,6 +101,13 @@
     far_m, near_m = (1 - zl) * 2 + c, zl * 2 + 1 - c
     far, near = (d, far_m), (d, near_m)
     spoke_m = (d + 3) % 4
+    is_hub = (d // 8 + spoke_m) % 2 == zl
+    order = lambda k: 2 + (k + 1) // 2 * (1 - 2 * (k % 2))
+
+    def spoke(j):
+        near_y, near_x, near_z = order(j // 4 % 4), order(j % 4), order(j // 16)
+        return (zh + near_z) % 4 * 32 + (x + near_x) % 4 * 8 + (y // 2 + near_y) % 4 * 2 + c
+
     mine = pl.ds(pl.multiple_of(m * 128, 128), 128)
     place = {"x": x, "y": y, "z": z, "u": (1 - c) * y + c * z, "v": c * y + (1 - c) * z}
     peer = {
@@ -124,10 +131,13 @@
         copy.start()
 
     def hello(j, _):
-        greet((4 * j + m, spoke_m))
+        greet((spoke(j), spoke_m))
         return 0
 
-    lax.fori_loop(0, HUBS, hello, 0)
+    @pl.when(is_hub)
+    def _():
+        lax.fori_loop(0, 64, hello, 0)
+
     greet(near)
     for axis in "xyz":
         for s in range(1, SIZE[axis]):
@@ -150,7 +160,9 @@
     pl.semaphore_wait(barrier, HUBS + 18)
 
     def leg1(i, _):
-        remote(pay.at[i], hub.at[d % 4, d // 4], send1, recv1, (4 * i + (m + 1) % 4, d % 4)).start()
+        i = (zh + order(i // 8)) % 4 * 8 + (x + order(i % 4)) % 4 * 2 + (y // 4 + 1 + i // 4) % 2
+        device = (4 * i + (m + 1) % 4, (i // 2 + m) % 2 * 2 + d % 2)
+        remote(pay.at[i], hub.at[d % 2, d // 2], send1, recv1, device).start()
         return 0
 
     lax.fori_loop(0, HUBS, leg1, 0)
@@ -165,7 +177,9 @@
         onehots(oh_src.at[:, lanes[k]], ids, 4 * k, 512)
         h = dot(own_b[...], oh_src[:, lanes[k]])
         h_s[:, lanes[k]] = h
-        q_s[:, lanes[k]] = complex_product(h, r_s[:, lanes[k]])
+        q = complex_product(h, r_s[:, lanes[k]])
+        q_s[:, lanes[k]] = q
+        qb_s[:, lanes[k]] = q.astype(bf16)
         onehots(oh_dst.at[:, lanes[k]], ids, 16 + 4 * k, 512)
 
     own_b[...] = emb[...].astype(bf16)
@@ -173,29 +187,26 @@
     rel3[0:400], rel3[400:800], rel3[800:1200] = split3(relations[...])
     gather_rel(oh_rel.at[:, lanes[0]], ids, 0, r_s)
 
-    drain(hub.at[m], recv1)
-    g_far = remote(hub.at[m], hub.at[m], gsend.at[0], grecv.at[0], far)
-    g_near = remote(hub.at[m], hub.at[m], gsend.at[1], grecv.at[1], near)
-    g_far.start()
-    g_near.start()
-    gather_rel(oh_rel.at[:, lanes[1]], ids, 1, r_s)
-    g_far.wait_recv()
-    g_fwd = remote(hub.at[far_m], hub.at[far_m], gsend.at[2], grecv.at[2], near)
-    g_fwd.start()
-    g_near.wait_recv()
-    g_fwd.wait_recv()
-
     def leg2(j, _):
-        t = 4 * j + m
+        t = spoke(j)
         p = partner_ref[t]
-        stage[j] = hub[p % 4, p // 4]
+        stage[j] = hub[p % 2, p // 2]
         remote(stage.at[j], got.at[d // 4], send2, recv2, (t, spoke_m)).start()
         return 0
 
-    lax.fori_loop(0, HUBS, leg2, 0)
+    @pl.when(is_hub)
+    def _():
+        drain(hub.at[c], recv1)
+        share = remote(hub.at[c], hub.at[c], gsend, grecv, near)
+        share.start()
+        share.wait()
+        lax.fori_loop(0, 64, leg2, 0)
+
+    gather_rel(oh_rel.at[:, lanes[1]], ids, 1, r_s)
     own_start(0)
     own_start(1)
-    count = [counts(ids, 24 + 8 * k) for k in range(2)]
+    for k in range(2):
+        cnt[k : k + 1, :] = counts(ids, 24 + 8 * k)
     drain(got, recv2)
 
     block = got.at[pl.ds(0, 25)]
@@ -203,30 +214,44 @@
     a_near = remote(block, cols.at[m], asend.at[1], arecv.at[1], near)
     a_far.start()
     a_near.start()
+
+    def place_cols(k, value):
+        other_b[:, pl.ds(pl.multiple_of(k * 128, 128), 128)] = value.reshape(400, 128)
+
+    def own_part(k, pair):
+        ents = pl.ds(pl.multiple_of(pair * 256, 256), 256)
+        part = other_b[:, ents]
+        t = dot(part, oh_dst[ents, lanes[k]])
+        negs = dot(part, qb_s[:, lanes[k]], 0, 0)
+        g = (jax.nn.sigmoid(negs) * 0.03125).astype(bf16)
+        weighted = part.astype(f32) * cnt[k : k + 1, ents]
+        w_hi = weighted.astype(bf16)
+        w_lo = (weighted - w_hi.astype(f32)).astype(bf16)
+        return t, dot(w_hi, g) + dot(w_lo, g)
+
+    place_cols(m, got[0:25])
     cols[m] = got[0:25]
     for a in range(ID_TILES):
         v = got[25 + a].astype(f32)
         pids[8 * a : 8 * a + 8, :] = (v[:8] * 32.0 + v[8:]).astype(i32)
     gather_rel(p_rel, pids, 0, pr_s)
+    a_near.wait_recv()
+    place_cols(near_m, cols[near_m])
+    for k in range(2):
+        t_s[:, lanes[k]], dq_s[:, lanes[k]] = own_part(k, zl)
     a_far.wait_recv()
     a_fwd = remote(cols.at[far_m], cols.at[far_m], asend.at[2], arecv.at[2], near)
     a_fwd.start()
+    place_cols(far_m, cols[far_m])
     gather_rel(p_rel, pids, 1, pr_s)
-    a_near.wait_recv()
     a_fwd.wait_recv()
-    for k in range(4):
-        other_b[:, 128 * k : 128 * (k + 1)] = cols[k].reshape(400, 128)
+    place_cols(3 - m, cols[3 - m])
 
     for k in range(2):
-        q = q_s[:, lanes[k]]
-        t = dot(other_b[...], oh_dst[:, lanes[k]])
-        g_pos = -jax.nn.sigmoid(-jnp.sum(q * t, axis=0, keepdims=True))
-        negs = dot(other_b[...], q.astype(bf16), 0, 0)
-        gt[...] = (jax.nn.sigmoid(negs) * 0.03125).astype(bf16)
-        weighted = other_b[...].astype(f32) * count[k]
-        w_hi = weighted.astype(bf16)
-        w_lo = (weighted - w_hi.astype(f32)).astype(bf16)
-        dq = t * g_pos + dot(w_hi, gt[...]) + dot(w_lo, gt[...])
+        t, back = own_part(k, 1 - zl)
+        t = t + t_s[:, lanes[k]]
+        g_pos = -jax.nn.sigmoid(-jnp.sum(q_s[:, lanes[k]] * t, axis=0, keepdims=True))
+        dq = t * g_pos + (dq_s[:, lanes[k]] + back)
         dq_s[:, lanes[k]] = dq
         for i, v in enumerate(split3(conj_product(dq, h_s[:, lanes[k]]))):
             dr3[400 * i : 400 * (i + 1), lanes[k]] = v
@@ -295,8 +320,9 @@
         elif level == 6:
             drain(ga.at[pl.ds(0, (na - 1) * n1)], rsem.at[i, 5])
             push(ga.at[pl.ds(0, T)], total.at[c, pl.ds(base, T)], near)
-            total[c, pl.ds(base, T)] = ga[0:T]
+            pltpu.make_async_copy(ga.at[pl.ds(0, T)], total.at[c, pl.ds(base, T)], osem.at[i]).start()
         else:
+            drain(in0, osem.at[i])
             drain(in0, rsem.at[i, 6])
             drain(in0, ssem.at[i, 0])
             drain(in1.at[pl.ds(0, na - 1)], ssem.at[i, 1])
@@ -360,61 +386,76 @@
         elif level == 4:
             drain(nblk.at[m], erecv.at[2])
             push(nblk.at[far_m], nblk.at[far_m], near)
-        else:
+        elif level == 5:
             drain(nblk.at[m], erecv.at[3])
             drain(nblk.at[m], erecv.at[4])
+            for k in range(4):
+                emb[:, 128 * k : 128 * (k + 1)] = nblk[k, 0:50].reshape(400, 128)
+                acc[:, 128 * k : 128 * (k + 1)] = nblk[k, 50, 0:1]
+            pltpu.make_async_copy(emb, nemb_out, osem.at[len(STREAMS)]).start()
+            pltpu.make_async_copy(acc, nacc_out, osem.at[len(STREAMS) + 1]).start()
+        else:
+            drain(emb, osem.at[len(STREAMS)])
+            drain(acc, osem.at[len(STREAMS) + 1])
             drain(e0, esend.at[0])
             drain(e1, esend.at[1])
             for k in range(2, 5):
                 drain(nblk.at[m], esend.at[k])
 
     rel_scatter(0)
+    step(0, 0)
     rel_scatter(1)
-    step(0, 0)
+    step(1, 0)
     rel_scatter(2)
-    step(1, 0)
+    step(2, 0)
     step(0, 1)
     rel_scatter(3)
-    step(2, 0)
+    step(3, 0)
     step(1, 1)
     step(2, 1)
+    step(3, 1)
     inputs[5].wait()
+    partner_a(0)
+    partner_b(0)
+    partner_a(1)
+    step(2, 2)
+    partner_b(1)
+    step(3, 2)
+    step(0, 2)
+    step(1, 2)
     dh(0)
     dh(1)
-    partner_a(0)
-    step(1, 2)
-    partner_b(0)
-    step(2, 2)
-    step(0, 2)
-    partner_a(1)
-    step(1, 3)
-    step(0, 3)
-    step(2, 3)
-    partner_b(1)
     ent_scatter(0)
-    step(1, 4)
-    step(0, 4)
     ent_scatter(1)
     ent(0)
-    step(2, 4)
-    step(1, 5)
-    step(0, 5)
+    step(2, 3)
+    step(0, 3)
+    step(1, 3)
+    step(3, 3)
     ent(1)
-    step(2, 5)
-    step(1, 6)
-    step(0, 6)
+    for i in (2, 0, 1, 3):
+        step(i, 4)
     ent(2)
     ent(3)
+    for i in (0, 1, 2, 3):
+        step(i, 5)
+    ent(4)
     step(2, 6)
-    ent(4)
+    step(0, 6)
     ent(5)
-    for i in range(3):
+    step(1, 6)
+    step(3, 6)
+    for i in range(4):
         step(i, 7)
-
-    for copy in (g_far, g_near, g_fwd, a_far, a_near, a_fwd):
+    ent(6)
+
+    for copy in (a_far, a_near, a_fwd):
         copy.wait_send()
     drain(pay, send1)
-    drain(stage, send2)
+
+    @pl.when(is_hub)
+    def _():
+        drain(stage, send2)
 
 
 def bucket_round(*args):
@@ -425,23 +466,28 @@
     scratch = [
         V((1, 1024), i32), V((1, 1024), i32), V((1, 1024), i32), V((1, 2, 1024), i32), V((400, 512), f32),
         V((1, 512), f32), V((400, 1024), f32), dma((7,)),
-        tile(32), tile(4, 32), tile(32), tile(32), tile(4, 25),
-        dma, dma, dma((3,)), dma((3,)), dma, dma, dma((3,)), dma((3,)),
+        tile(32), tile(2, 64), tile(64), tile(32), tile(4, 25), t(4, 51),
+        dma, dma, dma, dma, dma, dma, dma((3,)), dma((3,)),
         V((40, 128), i32), V((40, 128), i32), V((400, 512), bf16), V((400, 512), bf16), V((1200, 1024), bf16),
         V((512, 1024), bf16), V((512, 1024), bf16), V((1024, 1024), bf16),
         V((512, 512), bf16), V((512, 1024), bf16), V((1024, 512), bf16),
-        V((400, 1024), f32), V((400, 1024), f32), V((400, 1024), f32), V((400, 1024), f32), V((400, 1024), f32),
+        V((400, 1024), f32), V((400, 1024), f32), V((400, 1024), f32), V((400, 1024), bf16), V((400, 1024), f32),
+        V((400, 1024), f32), V((400, 1024), f32), V((8, 512), f32),
         V((1200, 1024), bf16), V((1200, 1024), bf16), V((512, 512), bf16), V((400, 512), f32),
         t(2, 200), t(4, 50),
-        t(2, 50), t(50), t(2, 50), dma((5,)), dma((5,)), dma((3, 7)), dma((3, 7)),
+        t(2, 50), t(50), t(2, 50), dma((5,)), dma((5,)), dma((len(STREAMS), 7)), dma((len(STREAMS), 7)), dma((len(STREAMS) + 2,)),
     ]
     for _, n, axes in STREAMS:
         scratch += stream_scratch(25 * n, axes)
     return pl.pallas_call(
         round_kernel,
-        out_shape=(jax.ShapeDtypeStruct((2, 200, 8, 128), f32), jax.ShapeDtypeStruct((4, 51, 8, 128), f32)),
+        out_shape=(
+            jax.ShapeDtypeStruct((2, 200, 8, 128), f32),
+            jax.ShapeDtypeStruct((400, 512), f32),
+            jax.ShapeDtypeStruct((1, 512), f32),
+        ),
         in_specs=[ANY] * 7 + [SMEM] * 2,
-        out_specs=(VMEM, VMEM),
+        out_specs=(ANY, ANY, ANY),
         scratch_shapes=scratch,
         compiler_params=pltpu.CompilerParams(
             collective_id=1, has_side_effects=True, vmem_limit_bytes=56 * 2**20
@@ -450,44 +496,73 @@
     )(*args)
 
 
-def update_kernel(total, nblk, rel_ref, racc_ref, nemb_ref, nacc_ref, nrel_ref, nracc_ref):
+def update_kernel(
+    total, nemb, nacc, rel_in, racc_in, nemb_out, nacc_out, nrel_out, nracc_out, g_v, rel_v, racc_v, emb_v, acc_v, sem
+):
+    copies = []
+
+    def move(src, dst):
+        copies.append(pltpu.make_async_copy(src, dst, sem.at[len(copies)]))
+        copies[-1].start()
+        return copies[-1]
+
+    rows = [slice(0, 200), slice(200, 400)]
+    fetch_g = [move(total.at[half], g_v.at[half]) for half in range(2)]
+    fetch_racc = move(racc_in, racc_v)
+    fetch_rel = [move(rel_in.at[rows[half]], rel_v.at[rows[half]]) for half in range(2)]
+    fetch_ent = [move(nemb, emb_v), move(nacc, acc_v)]
+    leave = []
+    squares = [jnp.zeros((8, 128), f32)] * 8
+    for half in range(2):
+        fetch_g[half].wait()
+        for k in range(8):
+            for i in range(25):
+                v = g_v[half, 25 * k + i]
+                squares[k] = squares[k] + v * v
+    for copy, src, dst in zip(fetch_ent, (emb_v, acc_v), (nemb_out, nacc_out)):
+        copy.wait()
+        leave.append(move(src, dst))
+    fetch_racc.wait()
+    rates = []
     for k in range(8):
         lanes = slice(128 * k, 128 * (k + 1))
-        square = jnp.zeros((8, 128), f32)
-        for half in range(2):
-            for i in range(25):
-                v = total[half, 25 * k + i]
-                square = square + v * v
-        new_racc = racc_ref[:, lanes] + jnp.sum(square, axis=0, keepdims=True) * (1.0 / 400.0)
-        rate = learn_rate / jnp.sqrt(new_racc)
-        nracc_ref[:, lanes] = new_racc
-        for half in range(2):
-            rows = slice(200 * half, 200 * (half + 1))
-            g = total[half, 25 * k : 25 * (k + 1)].reshape(200, 128)
-            nrel_ref[rows, lanes] = rel_ref[rows, lanes] - g * rate
-    for k in range(4):
-        lanes = slice(128 * k, 128 * (k + 1))
-        nemb_ref[:, lanes] = nblk[k, 0:50].reshape(400, 128)
-        nacc_ref[:, lanes] = nblk[k, 50, 0:1]
-
-
-def update(total, nblk, relations, racc):
+        new_racc = racc_v[:, lanes] + jnp.sum(squares[k], axis=0, keepdims=True) * (1.0 / 400.0)
+        rates.append(learn_rate / jnp.sqrt(new_racc))
+        racc_v[:, lanes] = new_racc
+    leave.append(move(racc_v, nracc_out))
+    for half in range(2):
+        fetch_rel[half].wait()
+        for k in range(8):
+            lanes = slice(128 * k, 128 * (k + 1))
+            g = g_v[half, 25 * k : 25 * (k + 1)].reshape(200, 128)
+            rel_v[rows[half], lanes] = rel_v[rows[half], lanes] - g * rates[k]
+        leave.append(move(rel_v.at[rows[half]], nrel_out.at[rows[half]]))
+    for copy in leave:
+        copy.wait()
+
+
+def update(total, nemb, nacc, relations, racc):
     shape = lambda *s: jax.ShapeDtypeStruct(s, f32)
+    V = pltpu.VMEM
     return pl.pallas_call(
         update_kernel,
         out_shape=(shape(400, 512), shape(1, 512), shape(400, 1024), shape(1, 1024)),
-        in_specs=[VMEM] * 4,
-        out_specs=(VMEM,) * 4,
-        compiler_params=pltpu.CompilerParams(vmem_limit_bytes=32 * 2**20),
+        in_specs=[ANY] * 5,
+        out_specs=(ANY,) * 4,
+        scratch_shapes=[
+            V((2, 200, 8, 128), f32), V((400, 1024), f32), V((1, 1024), f32),
+            V((400, 512), f32), V((1, 512), f32), pltpu.SemaphoreType.DMA((12,)),
+        ],
+        compiler_params=pltpu.CompilerParams(vmem_limit_bytes=60 * 2**20),
         name="update",
-    )(total, nblk, relations, racc)
+    )(total, nemb, nacc, relations, racc)
 
 
 def shards(embeddings, accum, relations, rel_accum, src_ids, rel_ids, dst_ids, neg_ids, bucket_len, partner):
-    total, nblk = bucket_round(
+    total, nemb, nacc = bucket_round(
         src_ids, rel_ids, dst_ids, neg_ids, embeddings, accum.reshape(1, 512), relations, bucket_len, partner
     )
-    new_emb, new_acc, new_rel, new_racc = update(total, nblk, relations, rel_accum.reshape(1, 1024))
+    new_emb, new_acc, new_rel, new_racc = update(total, nemb, nacc, relations, rel_accum.reshape(1, 1024))
     return new_emb, new_acc.reshape(512), new_rel, new_racc.reshape(1024)
 
 

time: 101 us -> 92.4 us (0.915)
  Pallas kernels: 96.4 us -> 90.7 us
  local copies, waits for them, and re-layouts: 2.58 us -> 0 us
    pallas_call x1, Pallas kernels: 94.5 us -> 87 us  [bucket_round(): pl.pallas_call(round_kernel, out_shape=(jax.ShapeDtypeStruct((2, 200, 8,...]
    unnamed x8 -> x0, local copies, waits for them, and re-layouts: 2.58 us -> none
    pallas_call x1, Pallas kernels: 1.95 us -> 3.69 us  [update(): pl.pallas_call(update_kernel, out_shape=(shape(400, 512), shape(1, 512),...]
where the time goes in v3:
time: 92.4 us; the launch traced here: 92.2 us
  Pallas kernels  90.7 us (98%)
  between operations  1.45 us (2%)
    pallas_call x1, Pallas kernels, bucket_round(): pl.pallas_call(round_kernel, out_shape=(jax.ShapeDtypeStruct((2, 200, 8,...  87 us
    pallas_call x1, Pallas kernels, update(): pl.pallas_call(update_kernel, out_shape=(shape(400, 512), shape(1, 512),...  3.69 us

profile of v3, /device:TPU:1, one launch (start us, length us, event | category | flops | bytes accessed | tf_op | source)
XLA Modules:
  0.0 92.2 jit_solution(11983183226803267824)
XLA Ops:
  1.3 87.0 %bucket_round.1 = (f32[2,200,8,128]{3,2,1,0:T(8,128)}, f32[400,512]{1,0:T(8,128)}, f32[1,512]{1,0:T(1,128)}) custom-call(s32[1,1024]{1,0:T(1,128)} %refs_0_.1, s32[1,1024]{1,0:T(1,128)} %refs_1_.1, s32[1,1024]{1,0:T(1,128)} %refs_2_.1, s32[1,2,1024]{2,1,0:T(2,128)} %refs_3_.1, f32[400,512]{1,0:T(8,128)} %refs_4_.1, f32[1,512]{1,0:T(1,128)} %bitcast.5, ...), custom_call_target="tpu_custom_call" | custom-call | tf_op jit(solution)/shard_map/bucket_round/pallas_call | solution.py:482
  88.3 3.7 %update.1 = (f32[400,512]{1,0:T(8,128)}, f32[1,512]{1,0:T(1,128)}, f32[400,1024]{1,0:T(8,128)}, f32[1,1024]{1,0:T(1,128)}) custom-call(f32[2,200,8,128]{3,2,1,0:T(8,128)} %get-tuple-element.11.total, f32[400,512]{1,0:T(8,128)} %get-tuple-element.12.nemb, f32[1,512]{1,0:T(1,128)} %get-tuple-element.13.nacc, f32[400,1024]{1,0:T(8,128)} %rel_in.1, ...), custom_call_target="tpu_custom_call" | custom-call | tf_op jit(solution)/shard_map/update/pallas_call | solution.py:547

commit v4 on v3

--- a/solution.py
+++ b/solution.py
@@ -14,7 +14,7 @@
 HUBS = 32
 ID_TILES = 5
 SIZE = {"x": 4, "y": 8, "z": 8, "u": 8, "v": 8}
-STREAMS = ((0, 2, "uxv"), (2, 2, "vxu"), (4, 2, "xyz"), (6, 2, "xzy"))
+STREAMS = ((0, 2, 'yxz'), (2, 3, 'xyz'), (5, 3, 'xzy'))
 
 
 def remote(src, dst, send, recv, device):
@@ -25,6 +25,10 @@
 
 def drain(ref, sem):
     pltpu.make_async_copy(ref, ref, sem).wait()
+
+
+def steps(size):
+    return sorted(range(1, size), key=lambda s: (-min(s, size - s), s))
 
 
 def levels(count, axes):
@@ -53,12 +57,21 @@
     return hi, mid, lo
 
 
+def split2(x):
+    hi = x.astype(bf16)
+    return hi, (x - hi.astype(f32)).astype(bf16)
+
+
 def dot(a, b, ca=1, cb=0):
     return lax.dot_general(a, b, (((ca,), (cb,)), ((), ())), preferred_element_type=f32)
 
 
 def add3(x):
     return x[0:400] + x[400:800] + x[800:1200]
+
+
+def add2(x):
+    return x[0:400] + x[400:800]
 
 
 def counts(ids, first):
@@ -89,7 +102,7 @@
     src_v, rel_v, dst_v, neg_v, emb, acc, relations, in_sem = take(8)
     pay, hub, stage, got, cols, nblk, send1, recv1, gsend, grecv, send2, recv2, asend, arecv = take(14)
     ids, pids, own_b, other_b, rel3, oh_src, oh_dst, oh_rel, p_src, p_dst, p_rel = take(11)
-    h_s, r_s, q_s, qb_s, t_s, dq_s, pr_s, cnt, dr3, parts, gt, dn, grel, grad = take(14)
+    h_s, r_s, q_s, qb_s, t_s, dq_s, pr_s, cnt, dr2, parts, gt, dn, grel, grad = take(14)
     e0, e1, hsum, esend, erecv, ssem, rsem, osem = take(8)
     streams = [(axes, 25 * n, 25 * lane, take(9)) for lane, n, axes in STREAMS]
 
@@ -253,11 +266,11 @@
         g_pos = -jax.nn.sigmoid(-jnp.sum(q_s[:, lanes[k]] * t, axis=0, keepdims=True))
         dq = t * g_pos + (dq_s[:, lanes[k]] + back)
         dq_s[:, lanes[k]] = dq
-        for i, v in enumerate(split3(conj_product(dq, h_s[:, lanes[k]]))):
-            dr3[400 * i : 400 * (i + 1), lanes[k]] = v
+        for i, v in enumerate(split2(conj_product(dq, h_s[:, lanes[k]]))):
+            dr2[400 * i : 400 * (i + 1), lanes[k]] = v
 
     def rel_scatter(n):
-        g = add3(dot(dr3[...], oh_rel[256 * n : 256 * (n + 1), :], 1, 1))
+        g = add2(dot(dr2[...], oh_rel[256 * n : 256 * (n + 1), :], 1, 1))
         for j in range(2):
             for half in range(2):
                 grel[half, pl.ds(25 * (2 * n + j), 25)] = g[
@@ -281,7 +294,7 @@
             a[0:T] = grel[c, pl.ds(base, T)] + in0[...]
             if na * n1 > T:
                 a[T : na * n1] = zeros(na * n1 - T)
-            for s in range(1, na):
+            for s in steps(na):
                 push(a.at[pl.ds(n1 * ((ma + s) % na), n1)], in1.at[ma], peer[A](s))
         elif level == 2:
             drain(in1.at[pl.ds(0, na - 1)], rsem.at[i, 1])
@@ -291,7 +304,7 @@
             b[0:n1] = v
             if nb * n2 > n1:
                 b[n1 : nb * n2] = zeros(nb * n2 - n1)
-            for s in range(1, nb):
+            for s in steps(nb):
                 push(b.at[pl.ds(n2 * ((mb + s) % nb), n2)], in2.at[mb], peer[B](s))
         elif level == 3:
             drain(in2.at[pl.ds(0, nb - 1)], rsem.at[i, 2])
@@ -300,7 +313,7 @@
                 v = v + in2[(mb + s) % nb]
             last[...] = v
             in3[mc] = v
-            for s in range(1, nc):
+            for s in steps(nc):
                 push(last, in3.at[mc], peer[C](s))
         elif level == 4:
             drain(in3.at[pl.ds(0, nc - 1)], rsem.at[i, 3])
@@ -309,12 +322,12 @@
                 v = v + in3[s]
             spot = pl.ds(n2 * mb, n2)
             gb[spot] = v
-            for s in range(1, nb):
+            for s in steps(nb):
                 push(gb.at[spot], gb.at[spot], peer[B](s))
         elif level == 5:
             drain(gb.at[pl.ds(0, (nb - 1) * n2)], rsem.at[i, 4])
             spot = pl.ds(n1 * ma, n1)
-            for s in range(1, na):
+            for s in steps(na):
                 push(gb.at[pl.ds(0, n1)], ga.at[spot], peer[A](s))
             ga[spot] = gb[0:n1]
         elif level == 6:
@@ -342,7 +355,7 @@
         q = complex_product(h, pr_s[:, lanes[k]])
         q_s[:, lanes[k]] = q
         g_pos = -jax.nn.sigmoid(-jnp.sum(q * t, axis=0, keepdims=True))
-        for i, v in enumerate(split3(q * g_pos)):
+        for i, v in enumerate(split2(q * g_pos)):
             parts[400 * i : 400 * (i + 1), lanes[k]] = v
 
     def partner_b(k):
@@ -352,12 +365,12 @@
         dn[...] = v if k == 0 else dn[...] + v
 
     def dh(k):
-        for i, v in enumerate(split3(conj_product(dq_s[:, lanes[k]], r_s[:, lanes[k]]))):
-            dr3[400 * i : 400 * (i + 1), lanes[k]] = v
+        for i, v in enumerate(split2(conj_product(dq_s[:, lanes[k]], r_s[:, lanes[k]]))):
+            dr2[400 * i : 400 * (i + 1), lanes[k]] = v
 
     def ent_scatter(n):
         rows = slice(256 * n, 256 * (n + 1))
-        g = add3(dot(dr3[...], oh_src[rows, :], 1, 1) + dot(parts[...], p_dst[rows, :], 1, 1)) + dn[:, rows]
+        g = add2(dot(dr2[...], oh_src[rows, :], 1, 1) + dot(parts[...], p_dst[rows, :], 1, 1)) + dn[:, rows]
         for j in range(2):
             grad[2 * n + j] = g[:, 128 * j : 128 * (j + 1)].reshape(50, 8, 128)
 
@@ -405,47 +418,44 @@
     rel_scatter(0)
     step(0, 0)
     rel_scatter(1)
+    rel_scatter(2)
     step(1, 0)
-    rel_scatter(2)
-    step(2, 0)
     step(0, 1)
     rel_scatter(3)
-    step(3, 0)
+    step(2, 0)
     step(1, 1)
     step(2, 1)
-    step(3, 1)
     inputs[5].wait()
     partner_a(0)
     partner_b(0)
     partner_a(1)
+    step(1, 2)
+    partner_b(1)
     step(2, 2)
-    partner_b(1)
-    step(3, 2)
     step(0, 2)
-    step(1, 2)
     dh(0)
     dh(1)
     ent_scatter(0)
     ent_scatter(1)
     ent(0)
+    step(1, 3)
+    step(0, 3)
     step(2, 3)
-    step(0, 3)
-    step(1, 3)
-    step(3, 3)
     ent(1)
-    for i in (2, 0, 1, 3):
-        step(i, 4)
+    step(1, 4)
+    step(0, 4)
+    step(2, 4)
     ent(2)
     ent(3)
-    for i in (0, 1, 2, 3):
-        step(i, 5)
+    step(0, 5)
+    step(1, 5)
+    step(2, 5)
     ent(4)
-    step(2, 6)
+    step(1, 6)
     step(0, 6)
     ent(5)
-    step(1, 6)
-    step(3, 6)
-    for i in range(4):
+    step(2, 6)
+    for i in range(3):
         step(i, 7)
     ent(6)
 
@@ -473,7 +483,7 @@
         V((512, 512), bf16), V((512, 1024), bf16), V((1024, 512), bf16),
         V((400, 1024), f32), V((400, 1024), f32), V((400, 1024), f32), V((400, 1024), bf16), V((400, 1024), f32),
         V((400, 1024), f32), V((400, 1024), f32), V((8, 512), f32),
-        V((1200, 1024), bf16), V((1200, 1024), bf16), V((512, 512), bf16), V((400, 512), f32),
+        V((800, 1024), bf16), V((800, 1024), bf16), V((512, 512), bf16), V((400, 512), f32),
         t(2, 200), t(4, 50),
         t(2, 50), t(50), t(2, 50), dma((5,)), dma((5,)), dma((len(STREAMS), 7)), dma((len(STREAMS), 7)), dma((len(STREAMS) + 2,)),
     ]

time: 92.4 us -> 88.2 us (0.955)
  Pallas kernels: 90.7 us -> 86.6 us
    pallas_call x1, Pallas kernels: 87 us -> 82.9 us  [bucket_round(): pl.pallas_call(round_kernel, out_shape=(jax.ShapeDtypeStruct((2, 200, 8,...]
where the time goes in v4:
time: 88.2 us; the launch traced here: 88 us
  Pallas kernels  86.6 us (98%)
  between operations  1.45 us (2%)
    pallas_call x1, Pallas kernels, bucket_round(): pl.pallas_call(round_kernel, out_shape=(jax.ShapeDtypeStruct((2, 200, 8,...  82.9 us
    pallas_call x1, Pallas kernels, update(): pl.pallas_call(update_kernel, out_shape=(shape(400, 512), shape(1, 512),...  3.69 us

profile of v4, /device:TPU:1, one launch (start us, length us, event | category | flops | bytes accessed | tf_op | source)
XLA Modules:
  0.0 88.0 jit_solution(8181759955475892124)
XLA Ops:
  1.3 82.9 %bucket_round.1 = (f32[2,200,8,128]{3,2,1,0:T(8,128)}, f32[400,512]{1,0:T(8,128)}, f32[1,512]{1,0:T(1,128)}) custom-call(s32[1,1024]{1,0:T(1,128)} %refs_0_.1, s32[1,1024]{1,0:T(1,128)} %refs_1_.1, s32[1,1024]{1,0:T(1,128)} %refs_2_.1, s32[1,2,1024]{2,1,0:T(2,128)} %refs_3_.1, f32[400,512]{1,0:T(8,128)} %refs_4_.1, f32[1,512]{1,0:T(1,128)} %bitcast.5, ...), custom_call_target="tpu_custom_call" | custom-call | tf_op jit(solution)/shard_map/bucket_round/pallas_call | solution.py:492
  84.2 3.7 %update.1 = (f32[400,512]{1,0:T(8,128)}, f32[1,512]{1,0:T(1,128)}, f32[400,1024]{1,0:T(8,128)}, f32[1,1024]{1,0:T(1,128)}) custom-call(f32[2,200,8,128]{3,2,1,0:T(8,128)} %get-tuple-element.11.total, f32[400,512]{1,0:T(8,128)} %get-tuple-element.12.nemb, f32[1,512]{1,0:T(1,128)} %get-tuple-element.13.nacc, f32[400,1024]{1,0:T(8,128)} %rel_in.1, ...), custom_call_target="tpu_custom_call" | custom-call | tf_op jit(solution)/shard_map/update/pallas_call | solution.py:557

commit v5 on v4

--- a/solution.py
+++ b/solution.py
@@ -14,7 +14,7 @@
 HUBS = 32
 ID_TILES = 5
 SIZE = {"x": 4, "y": 8, "z": 8, "u": 8, "v": 8}
-STREAMS = ((0, 2, 'yxz'), (2, 3, 'xyz'), (5, 3, 'xzy'))
+STREAMS = ((0, 3, 'xyz'), (3, 3, 'xzy'), (6, 2, 'yxz'))
 
 
 def remote(src, dst, send, recv, device):
@@ -199,6 +199,7 @@
     inputs[6].wait()
     rel3[0:400], rel3[400:800], rel3[800:1200] = split3(relations[...])
     gather_rel(oh_rel.at[:, lanes[0]], ids, 0, r_s)
+    own_start(0)
 
     def leg2(j, _):
         t = spoke(j)
@@ -216,7 +217,6 @@
         lax.fori_loop(0, 64, leg2, 0)
 
     gather_rel(oh_rel.at[:, lanes[1]], ids, 1, r_s)
-    own_start(0)
     own_start(1)
     for k in range(2):
         cnt[k : k + 1, :] = counts(ids, 24 + 8 * k)
@@ -416,8 +416,8 @@
                 drain(nblk.at[m], esend.at[k])
 
     rel_scatter(0)
+    rel_scatter(1)
     step(0, 0)
-    rel_scatter(1)
     rel_scatter(2)
     step(1, 0)
     step(0, 1)
@@ -429,32 +429,32 @@
     partner_a(0)
     partner_b(0)
     partner_a(1)
+    step(0, 2)
+    partner_b(1)
     step(1, 2)
-    partner_b(1)
     step(2, 2)
-    step(0, 2)
     dh(0)
     dh(1)
     ent_scatter(0)
     ent_scatter(1)
     ent(0)
+    step(0, 3)
     step(1, 3)
-    step(0, 3)
     step(2, 3)
     ent(1)
+    step(0, 4)
     step(1, 4)
-    step(0, 4)
     step(2, 4)
     ent(2)
     ent(3)
     step(0, 5)
+    step(2, 5)
     step(1, 5)
-    step(2, 5)
     ent(4)
+    step(0, 6)
+    step(2, 6)
+    ent(5)
     step(1, 6)
-    step(0, 6)
-    ent(5)
-    step(2, 6)
     for i in range(3):
         step(i, 7)
     ent(6)
@@ -517,11 +517,14 @@
         return copies[-1]
 
     rows = [slice(0, 200), slice(200, 400)]
+    fetch_ent = [move(nemb, emb_v), move(nacc, acc_v)]
     fetch_g = [move(total.at[half], g_v.at[half]) for half in range(2)]
     fetch_racc = move(racc_in, racc_v)
     fetch_rel = [move(rel_in.at[rows[half]], rel_v.at[rows[half]]) for half in range(2)]
-    fetch_ent = [move(nemb, emb_v), move(nacc, acc_v)]
     leave = []
+    for copy, src, dst in zip(fetch_ent, (emb_v, acc_v), (nemb_out, nacc_out)):
+        copy.wait()
+        leave.append(move(src, dst))
     squares = [jnp.zeros((8, 128), f32)] * 8
     for half in range(2):
         fetch_g[half].wait()
@@ -529,9 +532,6 @@
             for i in range(25):
                 v = g_v[half, 25 * k + i]
                 squares[k] = squares[k] + v * v
-    for copy, src, dst in zip(fetch_ent, (emb_v, acc_v), (nemb_out, nacc_out)):
-        copy.wait()
-        leave.append(move(src, dst))
     fetch_racc.wait()
     rates = []
     for k in range(8):

time: 88.2 us -> 87.7 us (level)
  no operation moved by 1% of the time
where the time goes in v5:
time: 87.7 us; the launch traced here: 87.5 us
  Pallas kernels  86 us (98%)
  between operations  1.47 us (2%)
    pallas_call x1, Pallas kernels, bucket_round(): pl.pallas_call(round_kernel, out_shape=(jax.ShapeDtypeStruct((2, 200, 8,...  82.5 us
    pallas_call x1, Pallas kernels, update(): pl.pallas_call(update_kernel, out_shape=(shape(400, 512), shape(1, 512),...  3.52 us

profile of v5, /device:TPU:1, one launch (start us, length us, event | category | flops | bytes accessed | tf_op | source)
XLA Modules:
  0.0 87.5 jit_solution(3061243533669281310)
XLA Ops:
  1.3 82.5 %bucket_round.1 = (f32[2,200,8,128]{3,2,1,0:T(8,128)}, f32[400,512]{1,0:T(8,128)}, f32[1,512]{1,0:T(1,128)}) custom-call(s32[1,1024]{1,0:T(1,128)} %refs_0_.1, s32[1,1024]{1,0:T(1,128)} %refs_1_.1, s32[1,1024]{1,0:T(1,128)} %refs_2_.1, s32[1,2,1024]{2,1,0:T(2,128)} %refs_3_.1, f32[400,512]{1,0:T(8,128)} %refs_4_.1, f32[1,512]{1,0:T(1,128)} %bitcast.5, ...), custom_call_target="tpu_custom_call" | custom-call | tf_op jit(solution)/shard_map/bucket_round/pallas_call | solution.py:492
  83.8 3.5 %update.1 = (f32[400,512]{1,0:T(8,128)}, f32[1,512]{1,0:T(1,128)}, f32[400,1024]{1,0:T(8,128)}, f32[1,1024]{1,0:T(1,128)}) custom-call(f32[2,200,8,128]{3,2,1,0:T(8,128)} %get-tuple-element.11.total, f32[400,512]{1,0:T(8,128)} %get-tuple-element.12.nemb, f32[1,512]{1,0:T(1,128)} %get-tuple-element.13.nacc, f32[400,1024]{1,0:T(8,128)} %rel_in.1, ...), custom_call_target="tpu_custom_call" | custom-call | tf_op jit(solution)/shard_map/update/pallas_call | solution.py:557
